TPU v7x, 256 devices: a whole 4x4x8 slice. The times are simulated.
256 devices in a mesh: vir: 64 (over y_hi, x, z), occ: 4 (over y_lo, core).
Axes of the slice: x: 4, y: 4 (y_hi: 2, y_lo: 2; y = y_hi * 2 + y_lo), z: 8, core: 2. Of those that a mesh axis runs over, the one named last changes fastest.
Arguments:
- l3_tiles: bfloat16 [64, 512, 128, 128], P('occ', 'vir'), may hold values from -6 to 6
- active: int32 [64, 512], P('occ', 'vir'), may hold values 0 or 1
- panels: bfloat16 [512, 128, 128], P('vir'), may hold values from -0.5 to 0.5
- coupling: float32 [512, 24], P('vir'), may hold values from -1.25 to 1.25
Outputs:
- r3_tiles: bfloat16 [64, 512, 128, 128], P('occ', 'vir')
- l2_block: bfloat16 [16, 128, 128], P('occ', 'vir')
All inputs are finite; a program needn't handle non-finite values. No bound on the sum of `active` on one device may be relied on, other than what follows from the above.
Results may differ from a plain program's by a relative error of at most 0.0049.
Values may be sent and summed in bfloat16 or wider, within the bound.
No kernel may reach another device: no remote copies, remote signals or barrier semaphores. Data moves between devices by JAX's collectives and lax.ppermute only.
A program may use at most 64 MiB of HBM per device.

v0:
```python
import jax
import jax.numpy as jnp
from jax import lax
from jax.sharding import PartitionSpec as P


def padded(x, sides, width):
    for axis, dim in sides:
        count, length = (lax.axis_size(axis), x.shape[dim])
        up = [(i, (i + 1) % count) for i in range(count)]
        down = [(j, i) for i, j in up]
        last = lax.slice_in_dim(x, length - width, length, axis=dim)
        first = lax.slice_in_dim(x, 0, width, axis=dim)
        before = lax.ppermute(last, axis, up)
        after = lax.ppermute(first, axis, down)
        x = jnp.concatenate([before, x, after], axis=dim)
    return x


def shards(l3_tiles, active, panels, coupling):
    width = panels.shape[1]
    pair_here = panels.shape[0]
    vir_count = lax.axis_size("vir")
    total_pairs = pair_here * vir_count
    rows = width // vir_count
    mask = active.astype(jnp.float32)
    masked_rows = l3_tiles * active.astype(jnp.bfloat16)[:, :, None, None]
    window = padded(panels, (("vir", 0),), pair_here)
    flat_window = window.reshape(3 * pair_here, width * width).astype(jnp.float32)
    combined_flat = jnp.dot(coupling, flat_window, precision=lax.Precision.HIGHEST)
    combined = combined_flat.reshape(pair_here, width, width).astype(jnp.bfloat16)
    partial_result = jnp.einsum(
        "zgqe,gei->zqi", masked_rows, panels, preferred_element_type=jnp.float32
    )
    summed = lax.psum(partial_result, "vir")
    meansq = jnp.mean(summed * summed, axis=(1, 2))
    normed_values = (summed * lax.rsqrt(meansq + 1e-05)[:, None, None]).astype(jnp.bfloat16)
    local_rows = lax.dynamic_slice_in_dim(summed, lax.axis_index("vir") * rows, rows, 1)
    direct = jnp.einsum("tpab,pbc->tpac", masked_rows, combined, preferred_element_type=jnp.float32)
    returned_rows = jnp.einsum(
        "bgx,fix->bfgi", normed_values, panels, preferred_element_type=jnp.float32
    )
    r3_tiles = (direct + mask[:, :, None, None] * returned_rows).astype(jnp.bfloat16)
    grouped_rows = lax.psum_scatter(local_rows, "occ", scatter_dimension=0, tiled=True)
    l2_block = (grouped_rows / jnp.sqrt(jnp.float32(total_pairs))).astype(jnp.bfloat16)
    return (r3_tiles, l2_block)


def solution(mesh):
    return jax.shard_map(
        shards,
        mesh=mesh,
        in_specs=(
            P("occ", "vir", None, None),
            P("occ", "vir"),
            P("vir", None, None),
            P("vir", None),
        ),
        out_specs=(P("occ", "vir", None, None), P("occ", "vir", None)),
        check_vma=False,
    )
```

profile of v0, /device:TPU:1, one launch (start us, length us, event | category | flops | bytes accessed | tf_op | source)
XLA Modules:
  0.0 746.2 jit_solution(7061567746014820439)
XLA Ops:
  7.2 0.0 copy-start
  7.2 0.0 all-reduce.3.cloned.1.call-start
  7.2 2.5 collective-permute-start
  9.8 8.9 %collective-permute-start.1 = (bf16[8,128,128]{2,1,0:T(8,128)(2,1)}, bf16[8,128,128]{2,1,0:T(8,128)(2,1)S(1)}, u32[]{:S(2)}, u32[]{:S(2)}) collective-permute-start(bf16[8,128,128]{2,1,0:T(8,128)(2,1)} %param.6), channel_id=1, source_target_pairs={{4,0},{8,4},{12,8},{16,12},{20,16},{24,20},{28,24},{32,28},{36,32}... | collective-permute-start | bytes 786440 | tf_op jit(solution)/shard_map/ppermute | solution.py:15
  18.6 0.8 fusion.13
  19.4 0.1 copy.11
  19.5 0.0 copy-start.2
  19.5 0.0 copy-start.1
  19.5 4.5 convolution_bitcast_fusion
  24.0 0.0 all-reduce.3.cloned.1.call-update
  24.0 0.0 copy-done.2
  24.0 0.6 dynamic-slice
  25.3 0.0 collective-permute-done
  25.3 0.0 collective-permute-done.1
  25.3 0.0 copy-done.1
  25.3 0.1 pad_maximum_fusion
  25.4 0.0 copy-done
  25.4 0.8 fusion.3
  26.2 6.8 fusion.1
  33.0 635.1 %all-reduce.3.cloned.1.call-done = f32[16,128,128]{2,1,0:T(8,128)} async-done(((f32[16,128,128]{2,1,0:T(8,128)}), f32[16,128,128]{2,1,0:T(8,128)}) %all-reduce.3.cloned.1.call-update) | async-done | bytes 1048592 | tf_op jit(solution)/shard_map/psum | solution.py:35
  668.1 1.4 multiply_reduce_fusion
  669.5 7.1 fusion
  676.6 6.4 copy.15
  683.0 0.8 constant_dynamic-slice_fusion
  683.9 54.9 %all-reduce = f32[16,2,128]{2,1,0:T(2,128)S(1)} all-reduce(f32[16,2,128]{2,1,0:T(2,128)S(1)} %constant_dynamic-slice_fusion), channel_id=2, replica_groups=mesh['vir'=64,'occ'=4] {'occ'}, use_global_device_ids=true, to_apply=%region_2.0.clone | all-reduce | flops 4096 | bytes 32768
  738.7 0.6 fusion.12
  (1 shorter events, 0.0 us)
Async XLA Ops:
  7.2 18.2 %copy-start = (f32[8,24]{1,0:T(8,128)S(1)}, f32[8,24]{1,0:T(8,128)}, u32[]{:S(2)}) copy-start(f32[8,24]{1,0:T(8,128)} %param.7) | copy-start | bytes 2308
  7.2 660.9 %all-reduce.3.cloned.1.call-start = ((), (), s32[]{:S(2)}) async-start(), calls=%async_computation | async-start | bytes 2097152 | tf_op jit(solution)/shard_map/psum | solution.py:35
  7.2 18.1 %collective-permute-start = (bf16[8,128,128]{2,1,0:T(8,128)(2,1)}, bf16[8,128,128]{2,1,0:T(8,128)(2,1)S(1)}, u32[]{:S(2)}, u32[]{:S(2)}) collective-permute-start(bf16[8,128,128]{2,1,0:T(8,128)(2,1)} %param.6), channel_id=1, source_target_pairs={{0,4},{4,8},{8,12},{12,16},{16,20},{20,24},{24,28},{28,32},{32,36}... | collective-permute-start | bytes 786440 | tf_op jit(solution)/shard_map/ppermute | solution.py:14
  9.8 15.5 %collective-permute-start.1 = (bf16[8,128,128]{2,1,0:T(8,128)(2,1)}, bf16[8,128,128]{2,1,0:T(8,128)(2,1)S(1)}, u32[]{:S(2)}, u32[]{:S(2)}) collective-permute-start(bf16[8,128,128]{2,1,0:T(8,128)(2,1)} %param.6), channel_id=1, source_target_pairs={{4,0},{8,4},{12,8},{16,12},{20,16},{24,20},{28,24},{32,28},{36,32}... | collective-permute-start | bytes 786440 | tf_op jit(solution)/shard_map/ppermute | solution.py:15
  19.5 4.6 copy-start.2
  19.5 5.8 copy-start.1
Sparse Core Ops, SparseCore 0:
  24.1 643.8 all-reduce.2
where the time goes:
time: 747 us; the launch traced here: 746 us
  waiting for transfers between devices  635 us (85%)
  blocking collectives  54.9 us (7%)
  matrix products  19.2 us (3%)
  between operations  14.8 us (2%)
  starting transfers between devices  11.4 us (2%)
  local copies, waits for them, and re-layouts  7.93 us (1%)
    psum x1, waiting for transfers between devices, shards(): summed = lax.psum(partial_result, 'vir')  635 us
    unnamed x1, blocking collectives  54.9 us
  transfers between devices with their start and end apart: 3, of which 1 were waited for; matrix products, arithmetic and copies ran while one was open for 2% of the time, Pallas kernels for 0%

commit v1 on v0

v1 whole, which is shorter than its diff:
```python
import functools

import jax
import jax.numpy as jnp
from jax import lax
from jax.experimental import pallas as pl
from jax.experimental.pallas import tpu as pltpu
from jax.sharding import PartitionSpec as P

VMEM_LIMIT = 40 * 1024 * 1024


def partial_kernel(active_ref, l3_ref, panels_ref, out_ref):
    block, pairs, width, _ = l3_ref.shape
    first = pl.program_id(0) * block
    weights = panels_ref[...].reshape(pairs * width, width)
    rows = []
    for t in range(block):
        tiles = [
            l3_ref[t, p] * active_ref[first + t, p].astype(jnp.float32).astype(jnp.bfloat16)
            for p in range(pairs)
        ]
        rows.append(jnp.concatenate(tiles, axis=1))
    lhs = jnp.concatenate(rows, axis=0)
    out_ref[...] = jnp.dot(lhs, weights, preferred_element_type=jnp.float32).astype(jnp.bfloat16)


def partial_sums(active, l3, panels, block=4):
    triples, pairs, width, _ = l3.shape
    return pl.pallas_call(
        partial_kernel,
        grid=(triples // block,),
        in_specs=[
            pl.BlockSpec(memory_space=pltpu.SMEM),
            pl.BlockSpec((block, pairs, width, width), lambda i: (i, 0, 0, 0)),
            pl.BlockSpec((pairs, width, width), lambda i: (0, 0, 0)),
        ],
        out_specs=pl.BlockSpec((block * width, width), lambda i: (i, 0)),
        out_shape=jax.ShapeDtypeStruct((triples * width, width), jnp.bfloat16),
        compiler_params=pltpu.CompilerParams(vmem_limit_bytes=VMEM_LIMIT),
        cost_estimate=pl.CostEstimate(
            flops=2 * triples * pairs * width**3, bytes_accessed=l3.size * 2, transcendentals=0
        ),
        name="partial_sums",
    )(active, l3, panels)


def total_kernel(parts_ref, out_ref):
    count = parts_ref.shape[0]
    total = parts_ref[0].astype(jnp.float32)
    for i in range(1, count):
        total = total + parts_ref[i].astype(jnp.float32)
    rounded = total.astype(jnp.bfloat16)
    for i in range(count):
        out_ref[i] = rounded


def total_copies(parts):
    return pl.pallas_call(
        total_kernel,
        in_specs=[pl.BlockSpec(memory_space=pltpu.VMEM)],
        out_specs=pl.BlockSpec(memory_space=pltpu.VMEM),
        out_shape=jax.ShapeDtypeStruct(parts.shape, jnp.bfloat16),
        cost_estimate=pl.CostEstimate(flops=parts.size, bytes_accessed=parts.size * 4, transcendentals=0),
        name="total_copies",
    )(parts)


def final_kernel(active_ref, l3_ref, summed_ref, combined_ref, panels_ref, out_ref, weights):
    block, pairs, width, _ = l3_ref.shape
    first = pl.program_id(0) * block

    @pl.when(pl.program_id(0) == 0)
    def _():
        for p in range(pairs):
            weights[p, :width] = combined_ref[p]
            weights[p, width:] = panels_ref[p].T

    normed = []
    for t in range(block):
        summed = summed_ref[t].astype(jnp.float32)
        meansq = jnp.sum(summed * summed) / (width * width)
        normed.append((summed * lax.rsqrt(meansq + 1e-05)).astype(jnp.bfloat16))
    for p in range(pairs):
        rows = []
        for t in range(block):
            mask = active_ref[first + t, p].astype(jnp.float32).astype(jnp.bfloat16)
            rows.append(jnp.concatenate([l3_ref[t, p] * mask, normed[t] * mask], axis=1))
        lhs = jnp.concatenate(rows, axis=0)
        tile = jnp.dot(lhs, weights[p], preferred_element_type=jnp.float32)
        out_ref[:, p] = tile.astype(jnp.bfloat16).reshape(block, width, width)


def residual(active, l3, summed, combined, panels, block=4):
    triples, pairs, width, _ = l3.shape
    return pl.pallas_call(
        final_kernel,
        grid=(triples // block,),
        in_specs=[
            pl.BlockSpec(memory_space=pltpu.SMEM),
            pl.BlockSpec((block, pairs, width, width), lambda i: (i, 0, 0, 0)),
            pl.BlockSpec((block, width, width), lambda i: (i, 0, 0)),
            pl.BlockSpec((pairs, width, width), lambda i: (0, 0, 0)),
            pl.BlockSpec((pairs, width, width), lambda i: (0, 0, 0)),
        ],
        out_specs=pl.BlockSpec((block, pairs, width, width), lambda i: (i, 0, 0, 0)),
        out_shape=jax.ShapeDtypeStruct(l3.shape, jnp.bfloat16),
        scratch_shapes=[pltpu.VMEM((pairs, 2 * width, width), jnp.bfloat16)],
        compiler_params=pltpu.CompilerParams(vmem_limit_bytes=VMEM_LIMIT),
        cost_estimate=pl.CostEstimate(
            flops=4 * triples * pairs * width**3, bytes_accessed=l3.size * 4, transcendentals=0
        ),
        name="residual",
    )(active, l3, summed, combined, panels)


def shards(l3_tiles, active, panels, coupling):
    triples, pairs, width, _ = l3_tiles.shape
    vir_count, occ_count = lax.axis_size("vir"), lax.axis_size("occ")
    rows = width // vir_count
    up = [(i, (i + 1) % vir_count) for i in range(vir_count)]
    down = [(j, i) for i, j in up]
    before = lax.ppermute(panels, "vir", up)
    after = lax.ppermute(panels, "vir", down)

    partial = partial_sums(active, l3_tiles, panels)
    parts = lax.all_to_all(partial.reshape(vir_count, -1, width), "vir", 0, 0, tiled=True)
    copies = total_copies(parts)
    summed = lax.all_to_all(copies, "vir", 0, 0, tiled=True).reshape(triples, width, width)

    window = jnp.concatenate([before, panels, after], axis=0)
    flat_window = window.reshape(3 * pairs, width * width).astype(jnp.float32)
    combined = jnp.dot(coupling, flat_window, precision=lax.Precision.HIGHEST)
    combined = combined.reshape(pairs, width, width).astype(jnp.bfloat16)

    local = lax.dynamic_slice_in_dim(summed, lax.axis_index("vir") * rows, rows, 1)
    local = local.astype(jnp.float32).reshape(occ_count, triples // occ_count, rows, width)
    groups = lax.all_to_all(local, "occ", 0, 0, tiled=True)
    r3_tiles = residual(active, l3_tiles, summed, combined, panels)
    total_pairs = pairs * vir_count
    l2_block = (jnp.sum(groups, axis=0) / jnp.sqrt(jnp.float32(total_pairs))).astype(jnp.bfloat16)
    return (r3_tiles, l2_block)


def solution(mesh):
    return jax.shard_map(
        shards,
        mesh=mesh,
        in_specs=(
            P("occ", "vir", None, None),
            P("occ", "vir"),
            P("vir", None, None),
            P("vir", None),
        ),
        out_specs=(P("occ", "vir", None, None), P("occ", "vir", None)),
        check_vma=False,
    )
```

time: 747 us -> 87.5 us (0.12)
  waiting for transfers between devices: 635 us -> 17 us
  blocking collectives: 54.9 us -> 32.5 us
  matrix products: 19.2 us -> 0.76 us
  between operations: 14.8 us -> 0.71 us
  Pallas kernels: 0 us -> 9.86 us
    psum x1 -> x0, waiting for transfers between devices: 635 us -> none  [shards(): summed = lax.psum(partial_result, 'vir')]
    unnamed x1 -> x0, blocking collectives: 54.9 us -> none
    all_to_all x0 -> x1, blocking collectives: none -> 32.5 us  [shards(): lax.all_to_all(partial.reshape(vir_count, -1, width), 'vir', 0, 0, tiled=...]
    dot_general x4 -> x1, matrix products: 19.2 us -> 0.76 us  [shards(): combined = jnp.dot(coupling, flat_window, precision=lax.Precision.HIGHEST)]
    ppermute x2, waiting for transfers between devices: 0.01 us -> 17 us  [the longest x1 10.5 us: shards(): after = lax.ppermute(panels, 'vir', down)]
    all_to_all x0 -> x2, starting transfers between devices: none -> 11.7 us  [the longest x1 7.09 us: shards(): lax.all_to_all(copies, 'vir', 0, 0, tiled=True)]
    pallas_call x0 -> x3, Pallas kernels: none -> 9.86 us  [the longest x1 5.44 us: residual(): pl.pallas_call(final_kernel, grid=(triples // block,), in_specs=[pl.Block...]
  transfers between devices with their start and end apart: 3 -> 4, of which waited for: 1 -> 2; matrix products, arithmetic and copies ran while one was open for 2% -> 1% of each run, Pallas kernels for 0% -> 6%
where the time goes in v1:
time: 87.5 us; the launch traced here: 87 us
  blocking collectives  32.5 us (37%)
  starting transfers between devices  18.8 us (21%)
  waiting for transfers between devices  17 us (19%)
  Pallas kernels  9.86 us (11%)
  local copies, waits for them, and re-layouts  6.16 us (7%)
  other arithmetic  1.29 us (1%)
    all_to_all x1, blocking collectives, shards(): lax.all_to_all(partial.reshape(vir_count, -1, width), 'vir', 0, 0, tiled=...  32.5 us
    ppermute x1, waiting for transfers between devices, shards(): after = lax.ppermute(panels, 'vir', down)  10.5 us
    ppermute x1, starting transfers between devices, shards(): after = lax.ppermute(panels, 'vir', down)  7.12 us
    all_to_all x1, starting transfers between devices, shards(): lax.all_to_all(copies, 'vir', 0, 0, tiled=True)  7.09 us
    ppermute x1, waiting for transfers between devices, shards(): before = lax.ppermute(panels, 'vir', up)  6.48 us
    unnamed x12, local copies, waits for them, and re-layouts  6.14 us
    pallas_call x1, Pallas kernels, residual(): pl.pallas_call(final_kernel, grid=(triples // block,), in_specs=[pl.Block...  5.44 us
    all_to_all x1, starting transfers between devices, shards(): groups = lax.all_to_all(local, 'occ', 0, 0, tiled=True)  4.6 us
  transfers between devices with their start and end apart: 4, of which 2 were waited for; matrix products, arithmetic and copies ran while one was open for 1% of the time, Pallas kernels for 6%

profile of v1, /device:TPU:1, one launch (start us, length us, event | category | flops | bytes accessed | tf_op | source)
XLA Modules:
  0.0 87.0 jit_solution(15789939254342764005)
XLA Ops:
  0.6 0.0 copy-start
  0.6 0.8 copy.7.active_ref
  1.4 0.0 copy-start.1
  1.4 2.2 %copy-done.1 = bf16[16,8,128,128]{3,2,1,0:T(8,128)(2,1)S(1)} copy-done((bf16[16,8,128,128]{3,2,1,0:T(8,128)(2,1)S(1)}, bf16[16,8,128,128]{3,2,1,0:T(8,128)(2,1)}, u32[]{:S(2)}) %copy-start.1) | copy-done | bytes 4194328
  3.6 0.0 copy-start.3
  3.6 0.9 %copy-done.3 = bf16[8,128,128]{2,1,0:T(8,128)(2,1)S(1)} copy-done((bf16[8,128,128]{2,1,0:T(8,128)(2,1)S(1)}, bf16[8,128,128]{2,1,0:T(8,128)(2,1)}, u32[]{:S(2)}) %copy-start.3) | copy-done | bytes 262168
  4.5 0.0 copy-start.4
  4.5 2.5 %partial_sums.1 = bf16[2048,128]{1,0:T(8,128)(2,1)S(1)} custom-call(s32[16,8]{1,0:T(8,128)S(1)} %copy.7.active_ref, bf16[16,8,128,128]{3,2,1,0:T(8,128)(2,1)S(1)} %copy-done.1, bf16[8,128,128]{2,1,0:T(8,128)(2,1)S(1)} %copy-done.3), custom_call_target="tpu_custom_call" | custom-call | flops 536870912 | bytes 4194304 | tf_op jit(solution)/shard_map/partial_sums/pallas_call | solution.py:30
  7.0 32.5 %all_to_all.15.parts_ref = bf16[64,32,128]{2,1,0:T(8,128)(2,1)} all-to-all(bf16[64,32,128]{2,1,0:T(8,128)(2,1)S(1)} %bitcast.17), channel_id=1, replica_groups=mesh['vir'=64,'occ'=4] {'vir'}, dimensions={0} | all-to-all | bytes 1048576 | tf_op jit(solution)/shard_map/all_to_all | solution.py:127
  39.5 1.9 %total_copies.1 = bf16[64,32,128]{2,1,0:T(8,128)(2,1)} custom-call(bf16[64,32,128]{2,1,0:T(8,128)(2,1)} %all_to_all.15.parts_ref), custom_call_target="tpu_custom_call" | custom-call | flops 262144 | bytes 1048576 | tf_op jit(solution)/shard_map/total_copies/pallas_call | solution.py:59
  41.4 7.1 %all-to-all-start.1 = ((bf16[64,32,128]{2,1,0:T(8,128)(2,1)}), bf16[64,32,128]{2,1,0:T(8,128)(2,1)S(1)}, u32[]{:S(2)}, u32[]{:S(2)}) async-start(bf16[64,32,128]{2,1,0:T(8,128)(2,1)} %total_copies.1), calls=%async_computation.1 | async-start | bytes 1048576 | tf_op jit(solution)/shard_map/all_to_all | solution.py:129
  48.5 0.0 copy-done.4
  48.5 7.1 %collective-permute-start.1 = (bf16[8,128,128]{2,1,0:T(8,128)(2,1)S(1)}, bf16[8,128,128]{2,1,0:T(8,128)(2,1)S(1)}, u32[]{:S(2)}, u32[]{:S(2)}) collective-permute-start(bf16[8,128,128]{2,1,0:T(8,128)(2,1)S(1)} %copy-done.4), channel_id=1, source_target_pairs={{4,0},{8,4},{12,8},{16,12},{20,16},{24,20},{28,24},{32,28},{36,32}... | collective-permute-start | bytes 786440 | tf_op jit(solution)/shard_map/ppermute | solution.py:124
  55.7 0.0 collective-permute-start
  55.7 10.5 %collective-permute-done.1 = bf16[8,128,128]{2,1,0:T(8,128)(2,1)S(1)} collective-permute-done((bf16[8,128,128]{2,1,0:T(8,128)(2,1)S(1)}, bf16[8,128,128]{2,1,0:T(8,128)(2,1)S(1)}, u32[]{:S(2)}, u32[]{:S(2)}) %collective-permute-start.1) | collective-permute-done | bytes 262176 | tf_op jit(solution)/shard_map/ppermute | solution.py:124
  66.2 6.5 %collective-permute-done = bf16[8,128,128]{2,1,0:T(8,128)(2,1)S(1)} collective-permute-done((bf16[8,128,128]{2,1,0:T(8,128)(2,1)S(1)}, bf16[8,128,128]{2,1,0:T(8,128)(2,1)S(1)}, u32[]{:S(2)}, u32[]{:S(2)}) %collective-permute-start) | collective-permute-done | bytes 262176 | tf_op jit(solution)/shard_map/ppermute | solution.py:123
  72.6 0.1 pad_maximum_fusion
  72.7 0.0 copy-done
  72.7 0.8 fusion
  73.5 0.0 all-to-all-done.1
  73.6 0.6 convert.1
  74.2 4.6 %all-to-all-start.2 = ((f32[4,4,2,128]{3,2,1,0:T(2,128)}), f32[4,4,2,128]{3,2,1,0:T(2,128)S(1)}, u32[]{:S(2)}, u32[]{:S(2)}) async-start(f32[4,4,2,128]{3,2,1,0:T(2,128)} %convert.1), calls=%async_computation.2 | async-start | bytes 32768 | tf_op jit(solution)/shard_map/all_to_all | solution.py:138
  78.8 0.0 copy-start.2
  78.8 2.2 %copy-done.2 = bf16[16,8,128,128]{3,2,1,0:T(8,128)(2,1)S(1)} copy-done((bf16[16,8,128,128]{3,2,1,0:T(8,128)(2,1)S(1)}, bf16[16,8,128,128]{3,2,1,0:T(8,128)(2,1)}, u32[]{:S(2)}) %copy-start.2) | copy-done | bytes 4194328
  81.0 5.4 %residual.1 = bf16[16,8,128,128]{3,2,1,0:T(8,128)(2,1)} custom-call(s32[16,8]{1,0:T(8,128)S(1)} %copy.7.active_ref, bf16[16,8,128,128]{3,2,1,0:T(8,128)(2,1)S(1)} %copy-done.2, bf16[16,128,128]{2,1,0:T(8,128)(2,1)S(1)} %bitcast.16, bf16[8,128,128]{2,1,0:T(8,128)(2,1)S(1)} %bitcast.18, bf16[8,128,128]{2,1,0:T(8,128)(2,1)S(1)} %copy-done.4), custom_call_target="tpu_custom_call" | custom-call | flops 1073741824 | bytes 8388608 | tf_op jit(solution)/shard_map/residual/pallas_call | solution.py:96
  86.4 0.0 all-to-all-done.2
  86.4 0.6 multiply_convert_fusion
  (3 shorter events, 0.1 us)
Async XLA Ops:
  0.6 72.1 %copy-start = (f32[8,24]{1,0:T(8,128)S(1)}, f32[8,24]{1,0:T(8,128)}, u32[]{:S(2)}) copy-start(f32[8,24]{1,0:T(8,128)} %param.7) | copy-start | bytes 2308
  1.4 2.2 %copy-start.1 = (bf16[16,8,128,128]{3,2,1,0:T(8,128)(2,1)S(1)}, bf16[16,8,128,128]{3,2,1,0:T(8,128)(2,1)}, u32[]{:S(2)}) copy-start(bf16[16,8,128,128]{3,2,1,0:T(8,128)(2,1)} %l3_ref.3) | copy-start | bytes 12582916
  3.6 0.9 %copy-start.3 = (bf16[8,128,128]{2,1,0:T(8,128)(2,1)S(1)}, bf16[8,128,128]{2,1,0:T(8,128)(2,1)}, u32[]{:S(2)}) copy-start(bf16[8,128,128]{2,1,0:T(8,128)(2,1)} %panels_ref.3) | copy-start | bytes 786436
  4.5 44.0 %copy-start.4 = (bf16[8,128,128]{2,1,0:T(8,128)(2,1)S(1)}, bf16[8,128,128]{2,1,0:T(8,128)(2,1)}, u32[]{:S(2)}) copy-start(bf16[8,128,128]{2,1,0:T(8,128)(2,1)} %panels_ref.3) | copy-start | bytes 786436
  41.4 32.1 %all-to-all-start.1 = ((bf16[64,32,128]{2,1,0:T(8,128)(2,1)}), bf16[64,32,128]{2,1,0:T(8,128)(2,1)S(1)}, u32[]{:S(2)}, u32[]{:S(2)}) async-start(bf16[64,32,128]{2,1,0:T(8,128)(2,1)} %total_copies.1), calls=%async_computation.1 | async-start | bytes 1048576 | tf_op jit(solution)/shard_map/all_to_all | solution.py:129
  48.5 17.6 %collective-permute-start.1 = (bf16[8,128,128]{2,1,0:T(8,128)(2,1)S(1)}, bf16[8,128,128]{2,1,0:T(8,128)(2,1)S(1)}, u32[]{:S(2)}, u32[]{:S(2)}) collective-permute-start(bf16[8,128,128]{2,1,0:T(8,128)(2,1)S(1)} %copy-done.4), channel_id=1, source_target_pairs={{4,0},{8,4},{12,8},{16,12},{20,16},{24,20},{28,24},{32,28},{36,32}... | collective-permute-start | bytes 786440 | tf_op jit(solution)/shard_map/ppermute | solution.py:124
  55.7 17.0 %collective-permute-start = (bf16[8,128,128]{2,1,0:T(8,128)(2,1)S(1)}, bf16[8,128,128]{2,1,0:T(8,128)(2,1)S(1)}, u32[]{:S(2)}, u32[]{:S(2)}) collective-permute-start(bf16[8,128,128]{2,1,0:T(8,128)(2,1)S(1)} %copy-done.4), channel_id=1, source_target_pairs={{0,4},{4,8},{8,12},{12,16},{16,20},{20,24},{24,28},{28,32},{32,36}... | collective-permute-start | bytes 786440 | tf_op jit(solution)/shard_map/ppermute | solution.py:123
  74.2 12.2 %all-to-all-start.2 = ((f32[4,4,2,128]{3,2,1,0:T(2,128)}), f32[4,4,2,128]{3,2,1,0:T(2,128)S(1)}, u32[]{:S(2)}, u32[]{:S(2)}) async-start(f32[4,4,2,128]{3,2,1,0:T(2,128)} %convert.1), calls=%async_computation.2 | async-start | bytes 32768 | tf_op jit(solution)/shard_map/all_to_all | solution.py:138
  78.8 2.2 %copy-start.2 = (bf16[16,8,128,128]{3,2,1,0:T(8,128)(2,1)S(1)}, bf16[16,8,128,128]{3,2,1,0:T(8,128)(2,1)}, u32[]{:S(2)}) copy-start(bf16[16,8,128,128]{3,2,1,0:T(8,128)(2,1)} %l3_ref.3) | copy-start | bytes 12582916

commit v2 on v0

v2 whole, which is shorter than its diff:
```python
import jax
import jax.numpy as jnp
from jax import lax
from jax.experimental import pallas as pl
from jax.experimental.pallas import tpu as pltpu
from jax.sharding import Mesh
from jax.sharding import PartitionSpec as P

MEDIUM = 16 * 1024 * 1024
LARGE = 60 * 1024 * 1024
SMALL = 4 * 1024 * 1024
VIR = ("yh", "x", "zh", "zl")
OCC = ("yl", "core")
NEAR = ("yh", "x", "zl")
EXTRA = 16


def params(limit):
    return pltpu.CompilerParams(vmem_limit_bytes=limit)


def whole(count):
    return [pl.BlockSpec(memory_space=pltpu.VMEM)] * count


def partial_kernel(flags_ref, l3_ref, panels_ref, out_ref, tiles_ref, held_ref, sems, *, block):
    triples, pairs, width, _ = l3_ref.shape
    loads = [
        pltpu.make_async_copy(l3_ref.at[t], tiles_ref.at[t], sems.at[t]) for t in range(triples)
    ]
    fetch = pltpu.make_async_copy(panels_ref, held_ref, sems.at[triples])
    fetch.start()
    for load in loads[: triples // 2]:
        load.start()
    fetch.wait()
    for load in loads[triples // 2 :]:
        load.start()
    weights = held_ref[...].reshape(pairs * width, width)
    for first in range(0, triples, block):
        rows = []
        for t in range(first, first + block):
            loads[t].wait()
            tiles = [
                tiles_ref[t, p] * flags_ref[p, t].astype(jnp.float32).astype(jnp.bfloat16)
                for p in range(pairs)
            ]
            rows.append(jnp.concatenate(tiles, axis=1))
        lhs = jnp.concatenate(rows, axis=0)
        sums = jnp.dot(lhs, weights, preferred_element_type=jnp.float32)
        out_ref[first * width : (first + block) * width] = sums.astype(jnp.bfloat16)


def partial_sums(flags, l3, panels, block=2):
    triples, pairs, width, _ = l3.shape

    def kernel(*refs):
        partial_kernel(*refs, block=block)

    return pl.pallas_call(
        kernel,
        in_specs=[
            pl.BlockSpec(memory_space=pltpu.SMEM),
            pl.BlockSpec(memory_space=pltpu.HBM),
            pl.BlockSpec(memory_space=pltpu.HBM),
        ],
        out_specs=whole(1)[0],
        out_shape=jax.ShapeDtypeStruct((triples * width, width), jnp.bfloat16),
        scratch_shapes=[
            pltpu.VMEM(l3.shape, jnp.bfloat16),
            pltpu.VMEM(panels.shape, jnp.bfloat16),
            pltpu.SemaphoreType.DMA((triples + 1,)),
        ],
        compiler_params=params(LARGE),
        cost_estimate=pl.CostEstimate(
            flops=2 * triples * pairs * width**3, bytes_accessed=l3.size * 2, transcendentals=0
        ),
        name="partial_sums",
    )(flags, l3, panels)


def add_up(parts_ref):
    total = parts_ref[0].astype(jnp.float32)
    for i in range(1, parts_ref.shape[0]):
        total = total + parts_ref[i].astype(jnp.float32)
    return total


def near_kernel(parts_ref, out_ref):
    rounded = add_up(parts_ref).astype(jnp.bfloat16)
    for i in range(out_ref.shape[0]):
        out_ref[i] = rounded


def near_sums(parts, count):
    return pl.pallas_call(
        near_kernel,
        in_specs=whole(1),
        out_specs=whole(1)[0],
        out_shape=jax.ShapeDtypeStruct((count, *parts.shape[1:]), jnp.bfloat16),
        compiler_params=params(SMALL),
        cost_estimate=pl.CostEstimate(flops=parts.size, bytes_accessed=parts.size * 4, transcendentals=0),
        name="near_sums",
    )(parts)


def normed_kernel(line_ref, parts_ref, out_ref, summed_ref, *, rows):
    _, chunk, width = parts_ref.shape
    count = out_ref.shape[0]
    summed_ref[...] = add_up(parts_ref)
    for first in range(0, chunk, width):
        tile = summed_ref[first : first + width]
        meansq = jnp.sum(tile * tile) / (width * width)
        normed = (tile * lax.rsqrt(meansq + 1e-05)).astype(jnp.bfloat16)
        for i in range(count):
            out_ref[i, first : first + width] = normed
    far = parts_ref.shape[0]
    for i in range(count):
        start = (i // 2 * 2 * far + line_ref[0] * 2 + i % 2) * rows
        own = [summed_ref[pl.ds(first + start, rows)] for first in range(0, chunk, width)]
        own = jnp.concatenate(own, axis=0)
        high = own.astype(jnp.bfloat16).astype(jnp.float32)
        zeros = jnp.zeros((EXTRA - 2 * own.shape[0], width), jnp.float32)
        pieces = jnp.concatenate([high, own - high, zeros], axis=0)
        out_ref[i, chunk:] = pieces.astype(jnp.bfloat16)


def normed_copies(parts, line, rows, count):
    _, chunk, width = parts.shape

    def kernel(*refs):
        normed_kernel(*refs, rows=rows)

    return pl.pallas_call(
        kernel,
        in_specs=[pl.BlockSpec(memory_space=pltpu.SMEM), *whole(1)],
        out_specs=whole(1)[0],
        out_shape=jax.ShapeDtypeStruct((count, chunk + EXTRA, width), jnp.bfloat16),
        scratch_shapes=[pltpu.VMEM((chunk, width), jnp.float32)],
        compiler_params=params(SMALL),
        cost_estimate=pl.CostEstimate(flops=parts.size, bytes_accessed=parts.size * 4, transcendentals=0),
        name="normed_copies",
    )(line, parts)


def weights_kernel(combined_ref, panels_ref, out_ref):
    pairs, width, _ = panels_ref.shape
    for p in range(pairs):
        out_ref[p, :width] = combined_ref[p]
        out_ref[p, width:] = panels_ref[p].T


def stacked_weights(combined, panels):
    pairs, width, _ = panels.shape
    return pl.pallas_call(
        weights_kernel,
        in_specs=whole(2),
        out_specs=whole(1)[0],
        out_shape=jax.ShapeDtypeStruct((pairs, 2 * width, width), jnp.bfloat16),
        compiler_params=params(SMALL),
        cost_estimate=pl.CostEstimate(flops=0, bytes_accessed=panels.size * 8, transcendentals=0),
        name="stacked_weights",
    )(combined, panels)


def final_kernel(flags_ref, l3_ref, normed_ref, weights_ref, r3_ref, out_ref, sems, *, block):
    triples, pairs, width, _ = l3_ref.shape
    held = triples // normed_ref.shape[0]
    stores = [pltpu.make_async_copy(out_ref.at[t], r3_ref.at[t], sems.at[t]) for t in range(triples)]
    for first in range(0, triples, block):
        here = range(first, first + block)
        normed = [normed_ref[t // held, t % held * width : (t % held + 1) * width] for t in here]
        for p in range(pairs):
            lhs = [jnp.concatenate([l3_ref[t, p], normed[t - first]], axis=1) for t in here]
            lhs = jnp.concatenate(lhs, axis=0)
            sums = jnp.dot(lhs, weights_ref[p], preferred_element_type=jnp.float32)
            for t in here:
                mask = flags_ref[p, t].astype(jnp.float32)
                tile = sums[(t - first) * width : (t - first + 1) * width] * mask
                out_ref[t, p] = tile.astype(jnp.bfloat16)
        for t in here:
            stores[t].start()
    for store in stores:
        store.wait()


def residual(flags, l3, normed, weights, block=2):
    triples, pairs, width, _ = l3.shape

    def kernel(*refs):
        final_kernel(*refs, block=block)

    return pl.pallas_call(
        kernel,
        in_specs=[pl.BlockSpec(memory_space=pltpu.SMEM), *whole(3)],
        out_specs=pl.BlockSpec(memory_space=pltpu.HBM),
        out_shape=jax.ShapeDtypeStruct(l3.shape, jnp.bfloat16),
        scratch_shapes=[
            pltpu.VMEM(l3.shape, jnp.bfloat16),
            pltpu.SemaphoreType.DMA((triples,)),
        ],
        compiler_params=params(MEDIUM),
        cost_estimate=pl.CostEstimate(
            flops=4 * triples * pairs * width**3, bytes_accessed=l3.size * 4, transcendentals=0
        ),
        name="residual",
    )(flags, l3, normed, weights)


def occ_sum(blocks):
    count = blocks.shape[0]
    me = lax.axis_index(OCC)
    total = lax.dynamic_index_in_dim(blocks, me, 0, keepdims=False)
    for step in range(1, count):
        sent = lax.dynamic_index_in_dim(blocks, me ^ step, 0, keepdims=False)
        total = total + lax.ppermute(sent, OCC, [(i, i ^ step) for i in range(count)])
    return total


def halo(panels):
    count = lax.axis_size(VIR)
    ring = [((v, 0), ((v + 1) % count, 0)) for v in range(count)]
    ring += [((v, 1), ((v - 1) % count, 1)) for v in range(count)]
    pairs = [(2 * v + c, 2 * w + d) for (v, c), (w, d) in ring]
    mine = lax.ppermute(panels, (*VIR, "core"), pairs)
    other = lax.ppermute(mine, "core", [(0, 1), (1, 0)])
    first = lax.axis_index("core") == 0
    return jnp.where(first, mine, other), jnp.where(first, other, mine)


def shards(l3_tiles, active, panels, coupling):
    triples, pairs, width, _ = l3_tiles.shape
    vir_count, occ_count = lax.axis_size(VIR), lax.axis_size(OCC)
    near, far = lax.axis_size(NEAR), lax.axis_size("zh")
    rows = width // vir_count
    flags = active.T
    partial = partial_sums(flags, l3_tiles, panels)
    before, after = halo(panels)
    parts = lax.all_to_all(partial.reshape(near, -1, width), NEAR, 0, 0, tiled=True)

    window = jnp.concatenate([before, panels, after], axis=0)
    flat_window = window.reshape(3 * pairs, width * width).astype(jnp.float32)
    combined = jnp.dot(coupling, flat_window, precision=lax.Precision.HIGHEST)
    combined = combined.reshape(pairs, width, width).astype(jnp.bfloat16)
    parts, combined = lax.optimization_barrier((parts, combined))

    copies, combined = lax.optimization_barrier((near_sums(parts, far), combined))
    parts = lax.all_to_all(copies, "zh", 0, 0, tiled=True)
    weights = stacked_weights(combined, panels)
    parts, weights = lax.optimization_barrier((parts, weights))

    line = lax.axis_index("zh").reshape(1)
    copies = normed_copies(parts, line, rows, near)
    gathered = lax.all_to_all(copies, NEAR, 0, 0, tiled=True)
    high_low = gathered[:, -EXTRA:][:, : 2 * triples // near * rows].astype(jnp.float32)
    high_low = high_low.reshape(near, 2, triples // near, rows, width)
    local = (high_low[:, 0] + high_low[:, 1]).reshape(occ_count, triples // occ_count, rows, width)
    total = occ_sum(local)
    r3_tiles = residual(flags, l3_tiles, gathered, weights)
    l2_block = (total / jnp.sqrt(jnp.float32(pairs * vir_count))).astype(jnp.bfloat16)
    return (r3_tiles, l2_block)


def solution(mesh):
    vir_count, occ_count = mesh.devices.shape
    split = mesh.devices.reshape(2, 4, vir_count // 16, 2, occ_count // 2, 2)
    return jax.shard_map(
        shards,
        mesh=Mesh(split, (*VIR, *OCC)),
        in_specs=(
            P(OCC, VIR, None, None),
            P(OCC, VIR),
            P(VIR, None, None),
            P(VIR, None),
        ),
        out_specs=(P(OCC, VIR, None, None), P(OCC, VIR, None)),
        check_vma=False,
    )
```

time: 747 us -> 68.1 us (0.09)
  waiting for transfers between devices: 635 us -> 23.6 us
  blocking collectives: 54.9 us -> 0 us
  matrix products: 19.2 us -> 0.76 us
  starting transfers between devices: 11.4 us -> 28.3 us
  between operations: 14.8 us -> 0.85 us
  Pallas kernels: 0 us -> 11.1 us
    psum x1 -> x0, waiting for transfers between devices: 635 us -> none  [shards(): summed = lax.psum(partial_result, 'vir')]
    unnamed x1 -> x0, blocking collectives: 54.9 us -> none
    all_to_all x0 -> x3, waiting for transfers between devices: none -> 22 us  [the longest x1 8.51 us: shards(): gathered = lax.all_to_all(copies, NEAR, 0, 0, tiled=True)]
    dot_general x4 -> x1, matrix products: 19.2 us -> 0.76 us  [shards(): combined = jnp.dot(coupling, flat_window, precision=lax.Precision.HIGHEST)]
    pallas_call x0 -> x5, Pallas kernels: none -> 11.1 us  [the longest x1 5.35 us: partial_sums(): pl.pallas_call(kernel, in_specs=[pl.BlockSpec(memory_space=pltpu.SMEM), p...]
    all_to_all x0 -> x3, starting transfers between devices: none -> 10.6 us  [the longest x1 3.66 us: shards(): gathered = lax.all_to_all(copies, NEAR, 0, 0, tiled=True)]
    ppermute x2 -> x5, starting transfers between devices: 11.4 us -> 17.7 us  [the longest x1 11.3 us: halo(): mine = lax.ppermute(panels, (*VIR, 'core'), pairs)]
  transfers between devices with their start and end apart: 3 -> 8, of which waited for: 1 -> 4; matrix products, arithmetic and copies ran while one was open for 2% -> 1% of each run, Pallas kernels for 0% -> 14%
where the time goes in v2:
time: 68.1 us; the launch traced here: 67.6 us
  starting transfers between devices  28.3 us (42%)
  waiting for transfers between devices  23.6 us (35%)
  Pallas kernels  11.1 us (16%)
  local copies, waits for them, and re-layouts  2.27 us (3%)
  between operations  0.85 us (1%)
  matrix products  0.76 us (1%)
  other arithmetic  0.75 us (1%)
    ppermute x1, starting transfers between devices, halo(): mine = lax.ppermute(panels, (*VIR, 'core'), pairs)  11.3 us
    all_to_all x1, waiting for transfers between devices, shards(): gathered = lax.all_to_all(copies, NEAR, 0, 0, tiled=True)  8.51 us
    all_to_all x1, waiting for transfers between devices, shards(): parts = lax.all_to_all(copies, 'zh', 0, 0, tiled=True)  7.42 us
    ppermute x3, starting transfers between devices, occ_sum(): lax.ppermute(sent, OCC, [(i, i ^ step) for i in range(count)])  6.34 us
    all_to_all x1, waiting for transfers between devices, shards(): lax.all_to_all(partial.reshape(near, -1, width), NEAR, 0, 0, tiled=True)  6.11 us
    pallas_call x1, Pallas kernels, partial_sums(): pl.pallas_call(kernel, in_specs=[pl.BlockSpec(memory_space=pltpu.SMEM), p...  5.35 us
    pallas_call x1, Pallas kernels, residual(): pl.pallas_call(kernel, in_specs=[pl.BlockSpec(memory_space=pltpu.SMEM), *...  3.88 us
    all_to_all x1, starting transfers between devices, shards(): gathered = lax.all_to_all(copies, NEAR, 0, 0, tiled=True)  3.66 us
  transfers between devices with their start and end apart: 8, of which 4 were waited for; matrix products, arithmetic and copies ran while one was open for 1% of the time, Pallas kernels for 14%

profile of v2, /device:TPU:1, one launch (start us, length us, event | category | flops | bytes accessed | tf_op | source)
XLA Modules:
  0.0 67.6 jit_solution(4055604853153363398)
XLA Ops:
  0.6 0.0 copy-start
  0.6 0.0 copy-start.2
  0.7 11.3 %collective-permute-start = (bf16[8,128,128]{2,1,0:T(8,128)(2,1)}, bf16[8,128,128]{2,1,0:T(8,128)(2,1)S(1)}, u32[]{:S(2)}, u32[]{:S(2)}) collective-permute-start(bf16[8,128,128]{2,1,0:T(8,128)(2,1)} %panels_ref.1), channel_id=1, source_target_pairs={{0,4},{4,8},{8,12},{12,16},{16,20},{20,24},{24,28},{28,32},{32,36}... | collective-permute-start | bytes 786440 | tf_op jit(solution)/shard_map/ppermute | solution.py:224
  12.0 5.3 %partial_sums.1 = bf16[2048,128]{1,0:T(8,128)(2,1)} custom-call(s32[8,16]{1,0:T(8,128)} %bitcast.34, bf16[16,8,128,128]{3,2,1,0:T(8,128)(2,1)} %refs_1_.3, bf16[8,128,128]{2,1,0:T(8,128)(2,1)} %panels_ref.1), custom_call_target="tpu_custom_call" | custom-call | flops 536870912 | bytes 4194304 | tf_op jit(solution)/shard_map/partial_sums/pallas_call | solution.py:59
  17.3 3.6 %all-to-all-start = ((bf16[16,128,128]{2,1,0:T(8,128)(2,1)}), bf16[16,128,128]{2,1,0:T(8,128)(2,1)S(1)}, u32[]{:S(2)}, u32[]{:S(2)}) async-start(bf16[16,128,128]{2,1,0:T(8,128)(2,1)} %bitcast.37), calls=%async_computation | async-start | bytes 1048576 | tf_op jit(solution)/shard_map/all_to_all | solution.py:238
  20.9 0.0 copy-start.3
  20.9 0.0 collective-permute-done
  20.9 0.1 collective-permute-start.1
  21.0 1.5 %collective-permute-done.1 = bf16[8,128,128]{2,1,0:T(8,128)(2,1)S(1)} collective-permute-done((bf16[8,128,128]{2,1,0:T(8,128)(2,1)S(1)}, bf16[8,128,128]{2,1,0:T(8,128)(2,1)S(1)}, u32[]{:S(2)}, u32[]{:S(2)}) %collective-permute-start.1) | collective-permute-done | bytes 262176 | tf_op jit(solution)/shard_map/ppermute | solution.py:225
  22.6 0.0 copy-done.2
  22.6 0.1 pad_maximum_fusion
  22.7 0.0 copy-done
  22.7 0.8 %fusion = bf16[1,8,128,128]{3,1,2,0:T(8,128)(2,1)S(1)} fusion(f32[8,24]{1,0:T(8,128)S(1)} %copy-done, bf16[3,8,128,128]{3,2,1,0:T(8,128)(2,1)S(1)} %bitcast.36), kind=kOutput, calls=%fused_computation.1 | convolution fusion | flops 37879808 | bytes 1049344 | tf_op jit(solution)/shard_map/dot_general | solution.py:242
  23.5 6.1 %all-to-all-done.parts_ref = bf16[16,128,128]{2,1,0:T(8,128)(2,1)S(1)} async-done(((bf16[16,128,128]{2,1,0:T(8,128)(2,1)}), bf16[16,128,128]{2,1,0:T(8,128)(2,1)S(1)}, u32[]{:S(2)}, u32[]{:S(2)}) %all-to-all-start) | async-done | bytes 524320 | tf_op jit(solution)/shard_map/all_to_all | solution.py:238
  29.6 0.7 %near_sums.1 = bf16[4,128,128]{2,1,0:T(8,128)(2,1)} custom-call(bf16[16,128,128]{2,1,0:T(8,128)(2,1)S(1)} %all-to-all-done.parts_ref), custom_call_target="tpu_custom_call" | custom-call | flops 262144 | bytes 1048576 | tf_op jit(solution)/shard_map/near_sums/pallas_call | solution.py:95
  30.4 3.3 %all-to-all-start.1 = ((bf16[4,128,128]{2,1,0:T(8,128)(2,1)}), bf16[4,128,128]{2,1,0:T(8,128)(2,1)S(1)}, u32[]{:S(2)}, u32[]{:S(2)}) async-start(bf16[4,128,128]{2,1,0:T(8,128)(2,1)} %near_sums.1), calls=%async_computation.1 | async-start | bytes 262144 | tf_op jit(solution)/shard_map/all_to_all | solution.py:247
  33.7 0.1 stacked_weights.1.refs_3_
  33.8 7.4 %all-to-all-done.1.refs_1_ = bf16[4,128,128]{2,1,0:T(8,128)(2,1)S(1)} async-done(((bf16[4,128,128]{2,1,0:T(8,128)(2,1)}), bf16[4,128,128]{2,1,0:T(8,128)(2,1)S(1)}, u32[]{:S(2)}, u32[]{:S(2)}) %all-to-all-start.1) | async-done | bytes 131104 | tf_op jit(solution)/shard_map/all_to_all | solution.py:247
  41.3 1.0 %normed_copies.1 = bf16[16,144,128]{2,1,0:T(8,128)(2,1)} custom-call(s32[1]{0:T(128)} %bitcast.1.refs_0_, bf16[4,128,128]{2,1,0:T(8,128)(2,1)S(1)} %all-to-all-done.1.refs_1_), custom_call_target="tpu_custom_call" | custom-call | flops 65536 | bytes 262144 | tf_op jit(solution)/shard_map/normed_copies/pallas_call | solution.py:133
  42.3 3.7 %all-to-all-start.2 = ((bf16[16,144,128]{2,1,0:T(8,128)(2,1)}), bf16[16,144,128]{2,1,0:T(8,128)(2,1)S(1)}, u32[]{:S(2)}, u32[]{:S(2)}) async-start(bf16[16,144,128]{2,1,0:T(8,128)(2,1)} %normed_copies.1), calls=%async_computation.2 | async-start | bytes 1179648 | tf_op jit(solution)/shard_map/all_to_all | solution.py:253
  46.0 8.5 %all-to-all-done.2.refs_2_ = bf16[16,144,128]{2,1,0:T(8,128)(2,1)S(1)} async-done(((bf16[16,144,128]{2,1,0:T(8,128)(2,1)}), bf16[16,144,128]{2,1,0:T(8,128)(2,1)S(1)}, u32[]{:S(2)}, u32[]{:S(2)}) %all-to-all-start.2) | async-done | bytes 589856 | tf_op jit(solution)/shard_map/all_to_all | solution.py:253
  54.6 5.3 %collective-permute-start.4 = (f32[4,2,128]{2,1,0:T(2,128)S(1)}, f32[4,2,128]{2,1,0:T(2,128)S(1)}, u32[]{:S(2)}, u32[]{:S(2)}) collective-permute-start(f32[4,2,128]{2,1,0:T(2,128)S(1)} %get-tuple-element.17), channel_id=1, source_target_pairs={{0,3},{1,2},{2,1},{3,0},{4,7},{5,6},{6,5},{7,4},{8,11},{9,10},{10,... | collective-permute-start | bytes 12296 | tf_op jit(solution)/shard_map/ppermute | solution.py:215
  59.8 1.1 %collective-permute-start.3 = (f32[4,2,128]{2,1,0:T(2,128)S(1)}, f32[4,2,128]{2,1,0:T(2,128)S(1)}, u32[]{:S(2)}, u32[]{:S(2)}) collective-permute-start(f32[4,2,128]{2,1,0:T(2,128)S(1)} %get-tuple-element.18), channel_id=1, source_target_pairs={{0,2},{1,3},{2,0},{3,1},{4,6},{5,7},{6,4},{7,5},{8,10},{9,11},{10,... | collective-permute-start | bytes 12296 | tf_op jit(solution)/shard_map/ppermute | solution.py:215
  60.9 0.0 collective-permute-start.2
  60.9 0.0 copy-done.3
  60.9 0.0 copy-start.1
  60.9 2.2 %copy-done.1 = bf16[16,8,128,128]{3,2,1,0:T(8,128)(2,1)S(1)} copy-done((bf16[16,8,128,128]{3,2,1,0:T(8,128)(2,1)S(1)}, bf16[16,8,128,128]{3,2,1,0:T(8,128)(2,1)}, u32[]{:S(2)}) %copy-start.1) | copy-done | bytes 4194328
  63.1 3.9 %residual.1 = bf16[16,8,128,128]{3,2,1,0:T(8,128)(2,1)} custom-call(s32[8,16]{1,0:T(8,128)S(1)} %bitcast.35, bf16[16,8,128,128]{3,2,1,0:T(8,128)(2,1)S(1)} %copy-done.1, bf16[16,144,128]{2,1,0:T(8,128)(2,1)S(1)} %all-to-all-done.2.refs_2_, bf16[8,256,128]{2,1,0:T(8,128)(2,1)S(1)} %stacked_weights.1.refs_3_), custom_call_target="tpu_custom_call" | custom-call | flops 1073741824 | bytes 8388608 | tf_op jit(solution)/shard_map/residual/pallas_call | solution.py:192
  67.0 0.0 collective-permute-done.4
  67.0 0.0 collective-permute-done.3
  67.0 0.0 collective-permute-done.2
  67.0 0.6 fusion.6
  (6 shorter events, 0.1 us)
Async XLA Ops:
  0.6 22.1 %copy-start = (f32[8,24]{1,0:T(8,128)S(1)}, f32[8,24]{1,0:T(8,128)}, u32[]{:S(2)}) copy-start(f32[8,24]{1,0:T(8,128)} %param.7) | copy-start | bytes 2308
  0.6 22.0 %copy-start.2 = (bf16[8,128,128]{2,1,0:T(8,128)(2,1)S(1)}, bf16[8,128,128]{2,1,0:T(8,128)(2,1)}, u32[]{:S(2)}) copy-start(bf16[8,128,128]{2,1,0:T(8,128)(2,1)} %panels_ref.1) | copy-start | bytes 786436
  0.7 20.3 %collective-permute-start = (bf16[8,128,128]{2,1,0:T(8,128)(2,1)}, bf16[8,128,128]{2,1,0:T(8,128)(2,1)S(1)}, u32[]{:S(2)}, u32[]{:S(2)}) collective-permute-start(bf16[8,128,128]{2,1,0:T(8,128)(2,1)} %panels_ref.1), channel_id=1, source_target_pairs={{0,4},{4,8},{8,12},{12,16},{16,20},{20,24},{24,28},{28,32},{32,36}... | collective-permute-start | bytes 786440 | tf_op jit(solution)/shard_map/ppermute | solution.py:224
  17.3 12.3 %all-to-all-start = ((bf16[16,128,128]{2,1,0:T(8,128)(2,1)}), bf16[16,128,128]{2,1,0:T(8,128)(2,1)S(1)}, u32[]{:S(2)}, u32[]{:S(2)}) async-start(bf16[16,128,128]{2,1,0:T(8,128)(2,1)} %bitcast.37), calls=%async_computation | async-start | bytes 1048576 | tf_op jit(solution)/shard_map/all_to_all | solution.py:238
  20.9 40.0 %copy-start.3 = (s32[16,8]{0,1:T(8,128)S(1)}, s32[16,8]{0,1:T(8,128)}, u32[]{:S(2)}) copy-start(s32[16,8]{0,1:T(8,128)} %param.5) | copy-start | bytes 1540
  20.9 1.6 %collective-permute-start.1 = (bf16[8,128,128]{2,1,0:T(8,128)(2,1)S(1)}, bf16[8,128,128]{2,1,0:T(8,128)(2,1)S(1)}, u32[]{:S(2)}, u32[]{:S(2)}) collective-permute-start(bf16[8,128,128]{2,1,0:T(8,128)(2,1)S(1)} %collective-permute-done), channel_id=1, source_target_pairs={{0,1},{1,0},{2,3},{3,2},{4,5},{5,4},{6,7},{7,6},{8,9},{9,8},{10,11... | collective-permute-start | bytes 786440 | tf_op jit(solution)/shard_map/ppermute | solution.py:225
  30.4 10.9 %all-to-all-start.1 = ((bf16[4,128,128]{2,1,0:T(8,128)(2,1)}), bf16[4,128,128]{2,1,0:T(8,128)(2,1)S(1)}, u32[]{:S(2)}, u32[]{:S(2)}) async-start(bf16[4,128,128]{2,1,0:T(8,128)(2,1)} %near_sums.1), calls=%async_computation.1 | async-start | bytes 262144 | tf_op jit(solution)/shard_map/all_to_all | solution.py:247
  42.3 12.2 %all-to-all-start.2 = ((bf16[16,144,128]{2,1,0:T(8,128)(2,1)}), bf16[16,144,128]{2,1,0:T(8,128)(2,1)S(1)}, u32[]{:S(2)}, u32[]{:S(2)}) async-start(bf16[16,144,128]{2,1,0:T(8,128)(2,1)} %normed_copies.1), calls=%async_computation.2 | async-start | bytes 1179648 | tf_op jit(solution)/shard_map/all_to_all | solution.py:253
  54.6 12.4 %collective-permute-start.4 = (f32[4,2,128]{2,1,0:T(2,128)S(1)}, f32[4,2,128]{2,1,0:T(2,128)S(1)}, u32[]{:S(2)}, u32[]{:S(2)}) collective-permute-start(f32[4,2,128]{2,1,0:T(2,128)S(1)} %get-tuple-element.17), channel_id=1, source_target_pairs={{0,3},{1,2},{2,1},{3,0},{4,7},{5,6},{6,5},{7,4},{8,11},{9,10},{10,... | collective-permute-start | bytes 12296 | tf_op jit(solution)/shard_map/ppermute | solution.py:215
  59.8 7.2 %collective-permute-start.3 = (f32[4,2,128]{2,1,0:T(2,128)S(1)}, f32[4,2,128]{2,1,0:T(2,128)S(1)}, u32[]{:S(2)}, u32[]{:S(2)}) collective-permute-start(f32[4,2,128]{2,1,0:T(2,128)S(1)} %get-tuple-element.18), channel_id=1, source_target_pairs={{0,2},{1,3},{2,0},{3,1},{4,6},{5,7},{6,4},{7,5},{8,10},{9,11},{10,... | collective-permute-start | bytes 12296 | tf_op jit(solution)/shard_map/ppermute | solution.py:215
  60.9 6.1 %collective-permute-start.2 = (f32[4,2,128]{2,1,0:T(2,128)S(1)}, f32[4,2,128]{2,1,0:T(2,128)S(1)}, u32[]{:S(2)}, u32[]{:S(2)}) collective-permute-start(f32[4,2,128]{2,1,0:T(2,128)S(1)} %get-tuple-element.16), channel_id=1, source_target_pairs={{0,1},{1,0},{2,3},{3,2},{4,5},{5,4},{6,7},{7,6},{8,9},{9,8},{10,11... | collective-permute-start | bytes 12296 | tf_op jit(solution)/shard_map/ppermute | solution.py:215
  60.9 2.2 %copy-start.1 = (bf16[16,8,128,128]{3,2,1,0:T(8,128)(2,1)S(1)}, bf16[16,8,128,128]{3,2,1,0:T(8,128)(2,1)}, u32[]{:S(2)}) copy-start(bf16[16,8,128,128]{3,2,1,0:T(8,128)(2,1)} %refs_1_.3) | copy-start | bytes 12582916

commit v3 on v2

--- a/solution.py
+++ b/solution.py
@@ -25,21 +25,21 @@
 
 def partial_kernel(flags_ref, l3_ref, panels_ref, out_ref, tiles_ref, held_ref, sems, *, block):
     triples, pairs, width, _ = l3_ref.shape
-    loads = [
-        pltpu.make_async_copy(l3_ref.at[t], tiles_ref.at[t], sems.at[t]) for t in range(triples)
-    ]
-    fetch = pltpu.make_async_copy(panels_ref, held_ref, sems.at[triples])
+    half = triples // 2
+    fetch = pltpu.make_async_copy(panels_ref, held_ref, sems.at[0])
     fetch.start()
-    for load in loads[: triples // 2]:
-        load.start()
+    loads = []
+    for i in range(2):
+        here = pl.ds(i * half, half)
+        loads.append(pltpu.make_async_copy(l3_ref.at[here], tiles_ref.at[here], sems.at[i + 1]))
+        loads[i].start()
     fetch.wait()
-    for load in loads[triples // 2 :]:
-        load.start()
     weights = held_ref[...].reshape(pairs * width, width)
     for first in range(0, triples, block):
+        if first % half == 0:
+            loads[first // half].wait()
         rows = []
         for t in range(first, first + block):
-            loads[t].wait()
             tiles = [
                 tiles_ref[t, p] * flags_ref[p, t].astype(jnp.float32).astype(jnp.bfloat16)
                 for p in range(pairs)
@@ -68,7 +68,7 @@
         scratch_shapes=[
             pltpu.VMEM(l3.shape, jnp.bfloat16),
             pltpu.VMEM(panels.shape, jnp.bfloat16),
-            pltpu.SemaphoreType.DMA((triples + 1,)),
+            pltpu.SemaphoreType.DMA((3,)),
         ],
         compiler_params=params(LARGE),
         cost_estimate=pl.CostEstimate(
@@ -78,42 +78,42 @@
     )(flags, l3, panels)
 
 
-def add_up(parts_ref):
-    total = parts_ref[0].astype(jnp.float32)
-    for i in range(1, parts_ref.shape[0]):
-        total = total + parts_ref[i].astype(jnp.float32)
+def add_up(parts):
+    total = parts[0][...].astype(jnp.float32)
+    for part in parts[1:]:
+        total = total + part[...].astype(jnp.float32)
     return total
 
 
 def near_kernel(parts_ref, out_ref):
-    rounded = add_up(parts_ref).astype(jnp.bfloat16)
-    for i in range(out_ref.shape[0]):
-        out_ref[i] = rounded
-
-
-def near_sums(parts, count):
+    parts = [parts_ref.at[i] for i in range(parts_ref.shape[0])]
+    out_ref[...] = add_up(parts).astype(jnp.bfloat16)
+
+
+def near_sums(parts):
     return pl.pallas_call(
         near_kernel,
         in_specs=whole(1),
         out_specs=whole(1)[0],
-        out_shape=jax.ShapeDtypeStruct((count, *parts.shape[1:]), jnp.bfloat16),
+        out_shape=jax.ShapeDtypeStruct(parts.shape[1:], jnp.bfloat16),
         compiler_params=params(SMALL),
         cost_estimate=pl.CostEstimate(flops=parts.size, bytes_accessed=parts.size * 4, transcendentals=0),
         name="near_sums",
     )(parts)
 
 
-def normed_kernel(line_ref, parts_ref, out_ref, summed_ref, *, rows):
-    _, chunk, width = parts_ref.shape
+def normed_kernel(line_ref, *refs, rows):
+    *parts, out_ref, summed_ref = refs
+    chunk, width = summed_ref.shape
     count = out_ref.shape[0]
-    summed_ref[...] = add_up(parts_ref)
+    summed_ref[...] = add_up(parts)
     for first in range(0, chunk, width):
         tile = summed_ref[first : first + width]
         meansq = jnp.sum(tile * tile) / (width * width)
         normed = (tile * lax.rsqrt(meansq + 1e-05)).astype(jnp.bfloat16)
         for i in range(count):
             out_ref[i, first : first + width] = normed
-    far = parts_ref.shape[0]
+    far = len(parts)
     for i in range(count):
         start = (i // 2 * 2 * far + line_ref[0] * 2 + i % 2) * rows
         own = [summed_ref[pl.ds(first + start, rows)] for first in range(0, chunk, width)]
@@ -125,41 +125,44 @@
 
 
 def normed_copies(parts, line, rows, count):
-    _, chunk, width = parts.shape
+    chunk, width = parts[0].shape
 
     def kernel(*refs):
         normed_kernel(*refs, rows=rows)
 
     return pl.pallas_call(
         kernel,
-        in_specs=[pl.BlockSpec(memory_space=pltpu.SMEM), *whole(1)],
+        in_specs=[pl.BlockSpec(memory_space=pltpu.SMEM), *whole(len(parts))],
         out_specs=whole(1)[0],
         out_shape=jax.ShapeDtypeStruct((count, chunk + EXTRA, width), jnp.bfloat16),
         scratch_shapes=[pltpu.VMEM((chunk, width), jnp.float32)],
         compiler_params=params(SMALL),
-        cost_estimate=pl.CostEstimate(flops=parts.size, bytes_accessed=parts.size * 4, transcendentals=0),
+        cost_estimate=pl.CostEstimate(
+            flops=4 * chunk * width, bytes_accessed=2 * count * chunk * width, transcendentals=0
+        ),
         name="normed_copies",
-    )(line, parts)
-
-
-def weights_kernel(combined_ref, panels_ref, out_ref):
+    )(line, *parts)
+
+
+def weights_kernel(l3_ref, combined_ref, panels_ref, out_ref):
+    del l3_ref
     pairs, width, _ = panels_ref.shape
     for p in range(pairs):
         out_ref[p, :width] = combined_ref[p]
         out_ref[p, width:] = panels_ref[p].T
 
 
-def stacked_weights(combined, panels):
+def stacked_weights(l3, combined, panels):
     pairs, width, _ = panels.shape
     return pl.pallas_call(
         weights_kernel,
-        in_specs=whole(2),
+        in_specs=whole(3),
         out_specs=whole(1)[0],
         out_shape=jax.ShapeDtypeStruct((pairs, 2 * width, width), jnp.bfloat16),
         compiler_params=params(SMALL),
         cost_estimate=pl.CostEstimate(flops=0, bytes_accessed=panels.size * 8, transcendentals=0),
         name="stacked_weights",
-    )(combined, panels)
+    )(l3, combined, panels)
 
 
 def final_kernel(flags_ref, l3_ref, normed_ref, weights_ref, r3_ref, out_ref, sems, *, block):
@@ -206,13 +209,21 @@
     )(flags, l3, normed, weights)
 
 
-def occ_sum(blocks):
+def own_indices():
+    me = lax.axis_index(OCC).astype(jnp.uint32)
+    return [me ^ jnp.uint32(step) for step in range(lax.axis_size(OCC))]
+
+
+def occ_sum(blocks, indices):
     count = blocks.shape[0]
-    me = lax.axis_index(OCC)
-    total = lax.dynamic_index_in_dim(blocks, me, 0, keepdims=False)
-    for step in range(1, count):
-        sent = lax.dynamic_index_in_dim(blocks, me ^ step, 0, keepdims=False)
-        total = total + lax.ppermute(sent, OCC, [(i, i ^ step) for i in range(count)])
+    zero = jnp.uint32(0)
+    total = None
+    for step, index in enumerate(indices):
+        starts = (index, *[zero] * (blocks.ndim - 1))
+        block = lax.dynamic_slice(blocks, starts, (1, *blocks.shape[1:]))[0]
+        if step:
+            block = lax.ppermute(block, OCC, [(i, i ^ step) for i in range(count)])
+        total = block if total is None else total + block
     return total
 
 
@@ -243,18 +254,21 @@
     combined = combined.reshape(pairs, width, width).astype(jnp.bfloat16)
     parts, combined = lax.optimization_barrier((parts, combined))
 
-    copies, combined = lax.optimization_barrier((near_sums(parts, far), combined))
-    parts = lax.all_to_all(copies, "zh", 0, 0, tiled=True)
-    weights = stacked_weights(combined, panels)
-    parts, weights = lax.optimization_barrier((parts, weights))
-
+    part, combined = lax.optimization_barrier((near_sums(parts), combined))
+    parts = [part]
+    for step in range(1, far):
+        parts.append(lax.ppermute(part, "zh", [(i, i ^ step) for i in range(far)]))
+    weights = stacked_weights(l3_tiles, combined, panels)
     line = lax.axis_index("zh").reshape(1)
+    indices = own_indices()
+    parts, weights, line, indices = lax.optimization_barrier((parts, weights, line, indices))
+
     copies = normed_copies(parts, line, rows, near)
     gathered = lax.all_to_all(copies, NEAR, 0, 0, tiled=True)
     high_low = gathered[:, -EXTRA:][:, : 2 * triples // near * rows].astype(jnp.float32)
     high_low = high_low.reshape(near, 2, triples // near, rows, width)
     local = (high_low[:, 0] + high_low[:, 1]).reshape(occ_count, triples // occ_count, rows, width)
-    total = occ_sum(local)
+    total = occ_sum(local, indices)
     r3_tiles = residual(flags, l3_tiles, gathered, weights)
     l2_block = (total / jnp.sqrt(jnp.float32(pairs * vir_count))).astype(jnp.bfloat16)
     return (r3_tiles, l2_block)

time: 68.1 us -> 62.5 us (0.918)
  waiting for transfers between devices: 23.6 us -> 7.63 us
  blocking collectives: 0 us -> 14.6 us
  Pallas kernels: 11.1 us -> 8.93 us
  starting transfers between devices: 28.3 us -> 26.4 us
    all_to_all x2 -> x0, waiting for transfers between devices: 15.9 us -> none  [the longest x1 8.51 us: shards(): gathered = lax.all_to_all(copies, NEAR, 0, 0, tiled=True)]
    all_to_all x0 -> x1, blocking collectives: none -> 14.6 us  [shards(): gathered = lax.all_to_all(copies, NEAR, 0, 0, tiled=True)]
    all_to_all x2 -> x0, starting transfers between devices: 6.99 us -> none  [the longest x1 3.66 us: shards(): gathered = lax.all_to_all(copies, NEAR, 0, 0, tiled=True)]
    ppermute x3 -> x6, starting transfers between devices: 6.34 us -> 11.5 us  [the longest x3 5.74 us: shards(): parts.append(lax.ppermute(part, 'zh', [(i, i ^ step) for i in range(far)]))]
    pallas_call x1, Pallas kernels: 1.04 us -> 0.23 us  [normed_copies(): pl.pallas_call(kernel, in_specs=[pl.BlockSpec(memory_space=pltpu.SMEM), *...]
    pallas_call x1, Pallas kernels: 5.35 us -> 4.64 us  [partial_sums(): pl.pallas_call(kernel, in_specs=[pl.BlockSpec(memory_space=pltpu.SMEM), p...]
    unnamed x9 -> x11, local copies, waits for them, and re-layouts: 2.25 us -> 2.25 us
  transfers between devices with their start and end apart: 8 -> 9, of which waited for: 4 -> 2; matrix products, arithmetic and copies ran while one was open for 1% -> 1% of each run, Pallas kernels for 14% -> 14%
where the time goes in v3:
time: 62.5 us; the launch traced here: 62.2 us
  starting transfers between devices  26.4 us (42%)
  blocking collectives  14.6 us (23%)
  Pallas kernels  8.93 us (14%)
  waiting for transfers between devices  7.63 us (12%)
  local copies, waits for them, and re-layouts  2.27 us (4%)
  between operations  0.84 us (1%)
  matrix products  0.76 us (1%)
  other arithmetic  0.74 us (1%)
    all_to_all x1, blocking collectives, shards(): gathered = lax.all_to_all(copies, NEAR, 0, 0, tiled=True)  14.6 us
    ppermute x1, starting transfers between devices, halo(): mine = lax.ppermute(panels, (*VIR, 'core'), pairs)  11.3 us
    all_to_all x1, waiting for transfers between devices, shards(): lax.all_to_all(partial.reshape(near, -1, width), NEAR, 0, 0, tiled=True)  6.1 us
    ppermute x3, starting transfers between devices, shards(): parts.append(lax.ppermute(part, 'zh', [(i, i ^ step) for i in range(far)]))  5.74 us
    ppermute x3, starting transfers between devices, occ_sum(): block = lax.ppermute(block, OCC, [(i, i ^ step) for i in range(count)])  5.72 us
    pallas_call x1, Pallas kernels, partial_sums(): pl.pallas_call(kernel, in_specs=[pl.BlockSpec(memory_space=pltpu.SMEM), p...  4.64 us
    pallas_call x1, Pallas kernels, residual(): pl.pallas_call(kernel, in_specs=[pl.BlockSpec(memory_space=pltpu.SMEM), *...  3.86 us
    all_to_all x1, starting transfers between devices, shards(): lax.all_to_all(partial.reshape(near, -1, width), NEAR, 0, 0, tiled=True)  3.59 us
  transfers between devices with their start and end apart: 9, of which 2 were waited for; matrix products, arithmetic and copies ran while one was open for 1% of the time, Pallas kernels for 14%

profile of v3, /device:TPU:1, one launch (start us, length us, event | category | flops | bytes accessed | tf_op | source)
XLA Modules:
  0.0 62.2 jit_solution(16866546824874952267)
XLA Ops:
  0.6 0.0 copy-start
  0.6 0.0 copy-start.3
  0.7 11.3 %collective-permute-start = (bf16[8,128,128]{2,1,0:T(8,128)(2,1)}, bf16[8,128,128]{2,1,0:T(8,128)(2,1)S(1)}, u32[]{:S(2)}, u32[]{:S(2)}) collective-permute-start(bf16[8,128,128]{2,1,0:T(8,128)(2,1)} %panels_ref.1), channel_id=1, source_target_pairs={{0,4},{4,8},{8,12},{12,16},{16,20},{20,24},{24,28},{28,32},{32,36}... | collective-permute-start | bytes 786440 | tf_op jit(solution)/shard_map/ppermute | solution.py:235
  12.0 4.6 %partial_sums.1 = bf16[2048,128]{1,0:T(8,128)(2,1)} custom-call(s32[8,16]{1,0:T(8,128)} %bitcast.34, bf16[16,8,128,128]{3,2,1,0:T(8,128)(2,1)} %refs_1_.3, bf16[8,128,128]{2,1,0:T(8,128)(2,1)} %panels_ref.1), custom_call_target="tpu_custom_call" | custom-call | flops 536870912 | bytes 4194304 | tf_op jit(solution)/shard_map/partial_sums/pallas_call | solution.py:59
  16.6 3.6 %all-to-all-start = ((bf16[16,128,128]{2,1,0:T(8,128)(2,1)}), bf16[16,128,128]{2,1,0:T(8,128)(2,1)S(1)}, u32[]{:S(2)}, u32[]{:S(2)}) async-start(bf16[16,128,128]{2,1,0:T(8,128)(2,1)} %bitcast.37), calls=%async_computation | async-start | bytes 1048576 | tf_op jit(solution)/shard_map/all_to_all | solution.py:249
  20.2 0.0 collective-permute-done
  20.2 0.1 collective-permute-start.1
  20.3 1.5 %collective-permute-done.1 = bf16[8,128,128]{2,1,0:T(8,128)(2,1)S(1)} collective-permute-done((bf16[8,128,128]{2,1,0:T(8,128)(2,1)S(1)}, bf16[8,128,128]{2,1,0:T(8,128)(2,1)S(1)}, u32[]{:S(2)}, u32[]{:S(2)}) %collective-permute-start.1) | collective-permute-done | bytes 262176 | tf_op jit(solution)/shard_map/ppermute | solution.py:236
  21.9 0.0 copy-done.3
  21.9 0.1 pad_maximum_fusion
  22.0 0.0 copy-done
  22.0 0.8 %fusion = bf16[1,8,128,128]{3,1,2,0:T(8,128)(2,1)S(1)} fusion(f32[8,24]{1,0:T(8,128)S(1)} %copy-done, bf16[3,8,128,128]{3,2,1,0:T(8,128)(2,1)S(1)} %bitcast.36), kind=kOutput, calls=%fused_computation.1 | convolution fusion | flops 37879808 | bytes 1049344 | tf_op jit(solution)/shard_map/dot_general | solution.py:253
  22.8 0.0 copy-start.4
  22.8 6.1 %all-to-all-done.parts_ref = bf16[16,128,128]{2,1,0:T(8,128)(2,1)S(1)} async-done(((bf16[16,128,128]{2,1,0:T(8,128)(2,1)}), bf16[16,128,128]{2,1,0:T(8,128)(2,1)S(1)}, u32[]{:S(2)}, u32[]{:S(2)}) %all-to-all-start) | async-done | bytes 524320 | tf_op jit(solution)/shard_map/all_to_all | solution.py:249
  28.9 0.1 near_sums.1.refs_1_
  29.0 1.3 %collective-permute-start.4 = (bf16[128,128]{1,0:T(8,128)(2,1)S(1)}, bf16[128,128]{1,0:T(8,128)(2,1)S(1)}, u32[]{:S(2)}, u32[]{:S(2)}) collective-permute-start(bf16[128,128]{1,0:T(8,128)(2,1)S(1)} %near_sums.1.refs_1_), channel_id=1, source_target_pairs={{0,24},{8,16},{16,8},{24,0},{1,25},{9,17},{17,9},{25,1},{2,26},{10... | collective-permute-start | bytes 98312 | tf_op jit(solution)/shard_map/ppermute | solution.py:260
  30.3 0.0 collective-permute-start.3
  30.3 4.4 %collective-permute-start.2 = (bf16[128,128]{1,0:T(8,128)(2,1)S(1)}, bf16[128,128]{1,0:T(8,128)(2,1)S(1)}, u32[]{:S(2)}, u32[]{:S(2)}) collective-permute-start(bf16[128,128]{1,0:T(8,128)(2,1)S(1)} %near_sums.1.refs_1_), channel_id=1, source_target_pairs={{0,8},{8,0},{16,24},{24,16},{1,9},{9,1},{17,25},{25,17},{2,10},{10... | collective-permute-start | bytes 98312 | tf_op jit(solution)/shard_map/ppermute | solution.py:260
  34.7 0.0 copy-start.1
  34.7 2.2 %copy-done.1 = bf16[16,8,128,128]{3,2,1,0:T(8,128)(2,1)S(1)} copy-done((bf16[16,8,128,128]{3,2,1,0:T(8,128)(2,1)S(1)}, bf16[16,8,128,128]{3,2,1,0:T(8,128)(2,1)}, u32[]{:S(2)}) %copy-start.1) | copy-done | bytes 4194328
  36.9 0.0 copy-start.2
  36.9 0.1 stacked_weights.1.refs_3_
  37.1 0.0 collective-permute-done.4.refs_4_
  37.1 0.0 collective-permute-done.3.refs_3_
  37.1 0.0 collective-permute-done.2.refs_2_
  37.1 0.2 normed_copies.1
  37.3 14.6 %all_to_all.10.refs_2_ = bf16[16,144,128]{2,1,0:T(8,128)(2,1)S(1)} all-to-all(bf16[16,144,128]{2,1,0:T(8,128)(2,1)S(1)} %normed_copies.1), channel_id=1, replica_groups=mesh['yh'=2,'x'=4,'zh'=4,'zl'=2,'yl'=2,'core'=2] {'yh','x','zl'}, dimensions={0} | all-to-all | bytes 1179648 | tf_op jit(solution)/shard_map/all_to_all | solution.py:267
  52.0 4.3 %collective-permute-start.5 = (f32[4,2,128]{2,1,0:T(2,128)S(1)}, f32[4,2,128]{2,1,0:T(2,128)S(1)}, u32[]{:S(2)}, u32[]{:S(2)}) collective-permute-start(f32[4,2,128]{2,1,0:T(2,128)S(1)} %get-tuple-element.32), channel_id=1, source_target_pairs={{0,1},{1,0},{2,3},{3,2},{4,5},{5,4},{6,7},{7,6},{8,9},{9,8},{10,11... | collective-permute-start | bytes 12296 | tf_op jit(solution)/shard_map/ppermute | solution.py:225
  56.3 0.4 collective-permute-start.7
  56.6 1.1 %collective-permute-start.6 = (f32[4,2,128]{2,1,0:T(2,128)S(1)}, f32[4,2,128]{2,1,0:T(2,128)S(1)}, u32[]{:S(2)}, u32[]{:S(2)}) collective-permute-start(f32[4,2,128]{2,1,0:T(2,128)S(1)} %get-tuple-element.34), channel_id=1, source_target_pairs={{0,2},{1,3},{2,0},{3,1},{4,6},{5,7},{6,4},{7,5},{8,10},{9,11},{10,... | collective-permute-start | bytes 12296 | tf_op jit(solution)/shard_map/ppermute | solution.py:225
  57.7 0.0 copy-done.4
  57.7 0.0 copy-done.2
  57.7 3.9 %residual.1 = bf16[16,8,128,128]{3,2,1,0:T(8,128)(2,1)} custom-call(s32[8,16]{1,0:T(8,128)S(1)} %bitcast.35, bf16[16,8,128,128]{3,2,1,0:T(8,128)(2,1)S(1)} %copy-done.2, bf16[16,144,128]{2,1,0:T(8,128)(2,1)S(1)} %all_to_all.10.refs_2_, bf16[8,256,128]{2,1,0:T(8,128)(2,1)S(1)} %stacked_weights.1.refs_3_), custom_call_target="tpu_custom_call" | custom-call | flops 1073741824 | bytes 8388608 | tf_op jit(solution)/shard_map/residual/pallas_call | solution.py:195
  61.6 0.0 collective-permute-done.5
  61.6 0.0 collective-permute-done.7
  61.6 0.0 collective-permute-done.6
  61.6 0.6 fusion.6
  (6 shorter events, 0.1 us)
Async XLA Ops:
  0.6 21.4 %copy-start = (f32[8,24]{1,0:T(8,128)S(1)}, f32[8,24]{1,0:T(8,128)}, u32[]{:S(2)}) copy-start(f32[8,24]{1,0:T(8,128)} %param.7) | copy-start | bytes 2308
  0.6 21.2 %copy-start.3 = (bf16[8,128,128]{2,1,0:T(8,128)(2,1)S(1)}, bf16[8,128,128]{2,1,0:T(8,128)(2,1)}, u32[]{:S(2)}) copy-start(bf16[8,128,128]{2,1,0:T(8,128)(2,1)} %panels_ref.1) | copy-start | bytes 786436
  0.7 19.6 %collective-permute-start = (bf16[8,128,128]{2,1,0:T(8,128)(2,1)}, bf16[8,128,128]{2,1,0:T(8,128)(2,1)S(1)}, u32[]{:S(2)}, u32[]{:S(2)}) collective-permute-start(bf16[8,128,128]{2,1,0:T(8,128)(2,1)} %panels_ref.1), channel_id=1, source_target_pairs={{0,4},{4,8},{8,12},{12,16},{16,20},{20,24},{24,28},{28,32},{32,36}... | collective-permute-start | bytes 786440 | tf_op jit(solution)/shard_map/ppermute | solution.py:235
  16.6 12.3 %all-to-all-start = ((bf16[16,128,128]{2,1,0:T(8,128)(2,1)}), bf16[16,128,128]{2,1,0:T(8,128)(2,1)S(1)}, u32[]{:S(2)}, u32[]{:S(2)}) async-start(bf16[16,128,128]{2,1,0:T(8,128)(2,1)} %bitcast.37), calls=%async_computation | async-start | bytes 1048576 | tf_op jit(solution)/shard_map/all_to_all | solution.py:249
  20.2 1.6 %collective-permute-start.1 = (bf16[8,128,128]{2,1,0:T(8,128)(2,1)S(1)}, bf16[8,128,128]{2,1,0:T(8,128)(2,1)S(1)}, u32[]{:S(2)}, u32[]{:S(2)}) collective-permute-start(bf16[8,128,128]{2,1,0:T(8,128)(2,1)S(1)} %collective-permute-done), channel_id=1, source_target_pairs={{0,1},{1,0},{2,3},{3,2},{4,5},{5,4},{6,7},{7,6},{8,9},{9,8},{10,11... | collective-permute-start | bytes 786440 | tf_op jit(solution)/shard_map/ppermute | solution.py:236
  22.8 34.9 %copy-start.4 = (s32[16,8]{0,1:T(8,128)S(1)}, s32[16,8]{0,1:T(8,128)}, u32[]{:S(2)}) copy-start(s32[16,8]{0,1:T(8,128)} %param.5) | copy-start | bytes 1540
  29.0 8.1 %collective-permute-start.4 = (bf16[128,128]{1,0:T(8,128)(2,1)S(1)}, bf16[128,128]{1,0:T(8,128)(2,1)S(1)}, u32[]{:S(2)}, u32[]{:S(2)}) collective-permute-start(bf16[128,128]{1,0:T(8,128)(2,1)S(1)} %near_sums.1.refs_1_), channel_id=1, source_target_pairs={{0,24},{8,16},{16,8},{24,0},{1,25},{9,17},{17,9},{25,1},{2,26},{10... | collective-permute-start | bytes 98312 | tf_op jit(solution)/shard_map/ppermute | solution.py:260
  30.3 6.7 %collective-permute-start.3 = (bf16[128,128]{1,0:T(8,128)(2,1)S(1)}, bf16[128,128]{1,0:T(8,128)(2,1)S(1)}, u32[]{:S(2)}, u32[]{:S(2)}) collective-permute-start(bf16[128,128]{1,0:T(8,128)(2,1)S(1)} %near_sums.1.refs_1_), channel_id=1, source_target_pairs={{0,16},{8,24},{16,0},{24,8},{1,17},{9,25},{17,1},{25,9},{2,18},{10... | collective-permute-start | bytes 98312 | tf_op jit(solution)/shard_map/ppermute | solution.py:260
  30.3 6.8 %collective-permute-start.2 = (bf16[128,128]{1,0:T(8,128)(2,1)S(1)}, bf16[128,128]{1,0:T(8,128)(2,1)S(1)}, u32[]{:S(2)}, u32[]{:S(2)}) collective-permute-start(bf16[128,128]{1,0:T(8,128)(2,1)S(1)} %near_sums.1.refs_1_), channel_id=1, source_target_pairs={{0,8},{8,0},{16,24},{24,16},{1,9},{9,1},{17,25},{25,17},{2,10},{10... | collective-permute-start | bytes 98312 | tf_op jit(solution)/shard_map/ppermute | solution.py:260
  34.7 2.2 %copy-start.1 = (bf16[16,8,128,128]{3,2,1,0:T(8,128)(2,1)S(1)}, bf16[16,8,128,128]{3,2,1,0:T(8,128)(2,1)}, u32[]{:S(2)}) copy-start(bf16[16,8,128,128]{3,2,1,0:T(8,128)(2,1)} %refs_1_.3) | copy-start | bytes 12582916
  36.9 20.8 %copy-start.2 = (bf16[16,8,128,128]{3,2,1,0:T(8,128)(2,1)S(1)}, bf16[16,8,128,128]{3,2,1,0:T(8,128)(2,1)}, u32[]{:S(2)}) copy-start(bf16[16,8,128,128]{3,2,1,0:T(8,128)(2,1)} %refs_1_.3) | copy-start | bytes 12582916
  52.0 9.6 %collective-permute-start.5 = (f32[4,2,128]{2,1,0:T(2,128)S(1)}, f32[4,2,128]{2,1,0:T(2,128)S(1)}, u32[]{:S(2)}, u32[]{:S(2)}) collective-permute-start(f32[4,2,128]{2,1,0:T(2,128)S(1)} %get-tuple-element.32), channel_id=1, source_target_pairs={{0,1},{1,0},{2,3},{3,2},{4,5},{5,4},{6,7},{7,6},{8,9},{9,8},{10,11... | collective-permute-start | bytes 12296 | tf_op jit(solution)/shard_map/ppermute | solution.py:225
  56.3 5.3 %collective-permute-start.7 = (f32[4,2,128]{2,1,0:T(2,128)S(1)}, f32[4,2,128]{2,1,0:T(2,128)S(1)}, u32[]{:S(2)}, u32[]{:S(2)}) collective-permute-start(f32[4,2,128]{2,1,0:T(2,128)S(1)} %get-tuple-element.33), channel_id=1, source_target_pairs={{0,3},{1,2},{2,1},{3,0},{4,7},{5,6},{6,5},{7,4},{8,11},{9,10},{10,... | collective-permute-start | bytes 12296 | tf_op jit(solution)/shard_map/ppermute | solution.py:225
  56.6 5.0 %collective-permute-start.6 = (f32[4,2,128]{2,1,0:T(2,128)S(1)}, f32[4,2,128]{2,1,0:T(2,128)S(1)}, u32[]{:S(2)}, u32[]{:S(2)}) collective-permute-start(f32[4,2,128]{2,1,0:T(2,128)S(1)} %get-tuple-element.34), channel_id=1, source_target_pairs={{0,2},{1,3},{2,0},{3,1},{4,6},{5,7},{6,4},{7,5},{8,10},{9,11},{10,... | collective-permute-start | bytes 12296 | tf_op jit(solution)/shard_map/ppermute | solution.py:225

commit v4 on v3

--- a/solution.py
+++ b/solution.py
@@ -23,31 +23,48 @@
     return [pl.BlockSpec(memory_space=pltpu.VMEM)] * count
 
 
-def partial_kernel(flags_ref, l3_ref, panels_ref, out_ref, tiles_ref, held_ref, sems, *, block):
+def partial_kernel(
+    flags_ref, l3_ref, panels_ref, partial_ref, flags, tiles, held, out, sems, out_sems, *, block
+):
     triples, pairs, width, _ = l3_ref.shape
     half = triples // 2
-    fetch = pltpu.make_async_copy(panels_ref, held_ref, sems.at[0])
-    fetch.start()
-    loads = []
-    for i in range(2):
-        here = pl.ds(i * half, half)
-        loads.append(pltpu.make_async_copy(l3_ref.at[here], tiles_ref.at[here], sems.at[i + 1]))
-        loads[i].start()
-    fetch.wait()
-    weights = held_ref[...].reshape(pairs * width, width)
+    fetches = [
+        pltpu.make_async_copy(flags_ref, flags, sems.at[0]),
+        pltpu.make_async_copy(panels_ref, held, sems.at[1]),
+    ]
+    loads = [
+        pltpu.make_async_copy(
+            l3_ref.at[pl.ds(i * half, half)], tiles.at[pl.ds(i * half, half)], sems.at[i + 2]
+        )
+        for i in range(2)
+    ]
+    for copy in (*fetches, *loads):
+        copy.start()
+    for copy in fetches:
+        copy.wait()
+    weights = held[...].reshape(pairs * width, width)
+    stores = []
     for first in range(0, triples, block):
         if first % half == 0:
             loads[first // half].wait()
         rows = []
         for t in range(first, first + block):
-            tiles = [
-                tiles_ref[t, p] * flags_ref[p, t].astype(jnp.float32).astype(jnp.bfloat16)
+            masked = [
+                tiles[t, p] * flags[p, t].astype(jnp.float32).astype(jnp.bfloat16)
                 for p in range(pairs)
             ]
-            rows.append(jnp.concatenate(tiles, axis=1))
+            rows.append(jnp.concatenate(masked, axis=1))
         lhs = jnp.concatenate(rows, axis=0)
         sums = jnp.dot(lhs, weights, preferred_element_type=jnp.float32)
-        out_ref[first * width : (first + block) * width] = sums.astype(jnp.bfloat16)
+        here = pl.ds(first * width, block * width)
+        out[here] = sums.astype(jnp.bfloat16)
+        store = pltpu.make_async_copy(
+            out.at[here], partial_ref.at[here], out_sems.at[first // block]
+        )
+        store.start()
+        stores.append(store)
+    for store in stores:
+        store.wait()
 
 
 def partial_sums(flags, l3, panels, block=2):
@@ -56,19 +73,19 @@
     def kernel(*refs):
         partial_kernel(*refs, block=block)
 
+    shape = (triples * width, width)
     return pl.pallas_call(
         kernel,
-        in_specs=[
-            pl.BlockSpec(memory_space=pltpu.SMEM),
-            pl.BlockSpec(memory_space=pltpu.HBM),
-            pl.BlockSpec(memory_space=pltpu.HBM),
-        ],
-        out_specs=whole(1)[0],
-        out_shape=jax.ShapeDtypeStruct((triples * width, width), jnp.bfloat16),
+        in_specs=[pl.BlockSpec(memory_space=pltpu.HBM)] * 3,
+        out_specs=pl.BlockSpec(memory_space=pltpu.HBM),
+        out_shape=jax.ShapeDtypeStruct(shape, jnp.bfloat16),
         scratch_shapes=[
+            pltpu.SMEM(flags.shape, jnp.int32),
             pltpu.VMEM(l3.shape, jnp.bfloat16),
             pltpu.VMEM(panels.shape, jnp.bfloat16),
-            pltpu.SemaphoreType.DMA((3,)),
+            pltpu.VMEM(shape, jnp.bfloat16),
+            pltpu.SemaphoreType.DMA((4,)),
+            pltpu.SemaphoreType.DMA((triples // block,)),
         ],
         compiler_params=params(LARGE),
         cost_estimate=pl.CostEstimate(
@@ -147,9 +164,17 @@
 def weights_kernel(l3_ref, combined_ref, panels_ref, out_ref):
     del l3_ref
     pairs, width, _ = panels_ref.shape
-    for p in range(pairs):
-        out_ref[p, :width] = combined_ref[p]
-        out_ref[p, width:] = panels_ref[p].T
+    zeros = jnp.zeros((width, width), jnp.bfloat16)
+    for k, p in enumerate(range(0, pairs, 4)):
+        for j, q in enumerate((p, p + 2)):
+            out_ref[3 * k + j, :width, :width] = combined_ref[q]
+            out_ref[3 * k + j, :width, width:] = zeros
+            out_ref[3 * k + j, width:, :width] = panels_ref[q].T
+            out_ref[3 * k + j, width:, width:] = panels_ref[q + 1].T
+        out_ref[3 * k + 2, :width, :width] = combined_ref[p + 1]
+        out_ref[3 * k + 2, :width, width:] = zeros
+        out_ref[3 * k + 2, width:, :width] = zeros
+        out_ref[3 * k + 2, width:, width:] = combined_ref[p + 3]
 
 
 def stacked_weights(l3, combined, panels):
@@ -158,9 +183,9 @@
         weights_kernel,
         in_specs=whole(3),
         out_specs=whole(1)[0],
-        out_shape=jax.ShapeDtypeStruct((pairs, 2 * width, width), jnp.bfloat16),
+        out_shape=jax.ShapeDtypeStruct((pairs // 4 * 3, 2 * width, 2 * width), jnp.bfloat16),
         compiler_params=params(SMALL),
-        cost_estimate=pl.CostEstimate(flops=0, bytes_accessed=panels.size * 8, transcendentals=0),
+        cost_estimate=pl.CostEstimate(flops=0, bytes_accessed=panels.size * 10, transcendentals=0),
         name="stacked_weights",
     )(l3, combined, panels)
 
@@ -169,17 +194,29 @@
     triples, pairs, width, _ = l3_ref.shape
     held = triples // normed_ref.shape[0]
     stores = [pltpu.make_async_copy(out_ref.at[t], r3_ref.at[t], sems.at[t]) for t in range(triples)]
+
+    def product(lhs, index):
+        lhs = jnp.concatenate([jnp.concatenate(row, axis=1) for row in lhs], axis=0)
+        return jnp.dot(lhs, weights_ref[index], preferred_element_type=jnp.float32)
+
     for first in range(0, triples, block):
         here = range(first, first + block)
         normed = [normed_ref[t // held, t % held * width : (t % held + 1) * width] for t in here]
-        for p in range(pairs):
-            lhs = [jnp.concatenate([l3_ref[t, p], normed[t - first]], axis=1) for t in here]
-            lhs = jnp.concatenate(lhs, axis=0)
-            sums = jnp.dot(lhs, weights_ref[p], preferred_element_type=jnp.float32)
+        for k, p in enumerate(range(0, pairs, 4)):
+            one = product([[l3_ref[t, p], normed[t - first]] for t in here], 3 * k)
+            two = product([[l3_ref[t, p + 2], normed[t - first]] for t in here], 3 * k + 1)
+            direct = product([[l3_ref[t, p + 1], l3_ref[t, p + 3]] for t in here], 3 * k + 2)
+            sums = [
+                one[:, :width],
+                one[:, width:] + direct[:, :width],
+                two[:, :width],
+                two[:, width:] + direct[:, width:],
+            ]
             for t in here:
-                mask = flags_ref[p, t].astype(jnp.float32)
-                tile = sums[(t - first) * width : (t - first + 1) * width] * mask
-                out_ref[t, p] = tile.astype(jnp.bfloat16)
+                for j in range(4):
+                    mask = flags_ref[p + j, t].astype(jnp.float32)
+                    tile = sums[j][(t - first) * width : (t - first + 1) * width] * mask
+                    out_ref[t, p + j] = tile.astype(jnp.bfloat16)
         for t in here:
             stores[t].start()
     for store in stores:

time: 62.5 us -> 61.1 us (0.978)
  Pallas kernels: 8.93 us -> 7.6 us
    pallas_call x1, Pallas kernels: 4.64 us -> 3.83 us  [partial_sums(): pl.pallas_call(kernel, in_specs=[pl.BlockSpec(memory_space=pltpu.HBM)] *...]
  transfers between devices with their start and end apart: 9 -> 9, of which waited for: 2 -> 2; matrix products, arithmetic and copies ran while one was open for 1% -> 2% of each run, Pallas kernels for 14% -> 12%
where the time goes in v4:
time: 61.1 us; the launch traced here: 60.9 us
  starting transfers between devices  26.4 us (43%)
  blocking collectives  14.6 us (24%)
  waiting for transfers between devices  7.64 us (13%)
  Pallas kernels  7.6 us (12%)
  local copies, waits for them, and re-layouts  2.27 us (4%)
  between operations  0.83 us (1%)
  matrix products  0.76 us (1%)
  other arithmetic  0.74 us (1%)
    all_to_all x1, blocking collectives, shards(): gathered = lax.all_to_all(copies, NEAR, 0, 0, tiled=True)  14.6 us
    ppermute x1, starting transfers between devices, halo(): mine = lax.ppermute(panels, (*VIR, 'core'), pairs)  11.3 us
    all_to_all x1, waiting for transfers between devices, shards(): lax.all_to_all(partial.reshape(near, -1, width), NEAR, 0, 0, tiled=True)  6.1 us
    ppermute x3, starting transfers between devices, shards(): parts.append(lax.ppermute(part, 'zh', [(i, i ^ step) for i in range(far)]))  5.74 us
    ppermute x3, starting transfers between devices, occ_sum(): block = lax.ppermute(block, OCC, [(i, i ^ step) for i in range(count)])  5.72 us
    pallas_call x1, Pallas kernels, partial_sums(): pl.pallas_call(kernel, in_specs=[pl.BlockSpec(memory_space=pltpu.HBM)] *...  3.83 us
    all_to_all x1, starting transfers between devices, shards(): lax.all_to_all(partial.reshape(near, -1, width), NEAR, 0, 0, tiled=True)  3.59 us
    pallas_call x1, Pallas kernels, residual(): pl.pallas_call(kernel, in_specs=[pl.BlockSpec(memory_space=pltpu.SMEM), *...  3.34 us
  transfers between devices with their start and end apart: 9, of which 2 were waited for; matrix products, arithmetic and copies ran while one was open for 2% of the time, Pallas kernels for 12%

profile of v4, /device:TPU:1, one launch (start us, length us, event | category | flops | bytes accessed | tf_op | source)
XLA Modules:
  0.0 60.9 jit_solution(13307005377041940305)
XLA Ops:
  0.6 0.0 copy-start
  0.6 0.0 copy-start.3
  0.7 11.3 %collective-permute-start = (bf16[8,128,128]{2,1,0:T(8,128)(2,1)}, bf16[8,128,128]{2,1,0:T(8,128)(2,1)S(1)}, u32[]{:S(2)}, u32[]{:S(2)}) collective-permute-start(bf16[8,128,128]{2,1,0:T(8,128)(2,1)} %panels_ref.1), channel_id=1, source_target_pairs={{0,4},{4,8},{8,12},{12,16},{16,20},{20,24},{24,28},{28,32},{32,36}... | collective-permute-start | bytes 786440 | tf_op jit(solution)/shard_map/ppermute | solution.py:272
  12.0 3.8 %partial_sums.1 = bf16[2048,128]{1,0:T(8,128)(2,1)} custom-call(s32[8,16]{1,0:T(8,128)} %bitcast.34, bf16[16,8,128,128]{3,2,1,0:T(8,128)(2,1)} %refs_1_.3, bf16[8,128,128]{2,1,0:T(8,128)(2,1)} %panels_ref.1), custom_call_target="tpu_custom_call" | custom-call | flops 536870912 | bytes 4194304 | tf_op jit(solution)/shard_map/partial_sums/pallas_call | solution.py:77
  15.8 3.6 %all-to-all-start = ((bf16[16,128,128]{2,1,0:T(8,128)(2,1)}), bf16[16,128,128]{2,1,0:T(8,128)(2,1)S(1)}, u32[]{:S(2)}, u32[]{:S(2)}) async-start(bf16[16,128,128]{2,1,0:T(8,128)(2,1)} %bitcast.37), calls=%async_computation | async-start | bytes 1048576 | tf_op jit(solution)/shard_map/all_to_all | solution.py:286
  19.4 0.0 collective-permute-done
  19.4 0.1 collective-permute-start.1
  19.5 1.5 %collective-permute-done.1 = bf16[8,128,128]{2,1,0:T(8,128)(2,1)S(1)} collective-permute-done((bf16[8,128,128]{2,1,0:T(8,128)(2,1)S(1)}, bf16[8,128,128]{2,1,0:T(8,128)(2,1)S(1)}, u32[]{:S(2)}, u32[]{:S(2)}) %collective-permute-start.1) | collective-permute-done | bytes 262176 | tf_op jit(solution)/shard_map/ppermute | solution.py:273
  21.1 0.0 copy-done.3
  21.1 0.1 pad_maximum_fusion
  21.2 0.0 copy-done
  21.2 0.8 %fusion = bf16[1,8,128,128]{3,1,2,0:T(8,128)(2,1)S(1)} fusion(f32[8,24]{1,0:T(8,128)S(1)} %copy-done, bf16[3,8,128,128]{3,2,1,0:T(8,128)(2,1)S(1)} %bitcast.36), kind=kOutput, calls=%fused_computation.1 | convolution fusion | flops 37879808 | bytes 1049344 | tf_op jit(solution)/shard_map/dot_general | solution.py:290
  22.0 0.0 copy-start.4
  22.0 6.1 %all-to-all-done.parts_ref = bf16[16,128,128]{2,1,0:T(8,128)(2,1)S(1)} async-done(((bf16[16,128,128]{2,1,0:T(8,128)(2,1)}), bf16[16,128,128]{2,1,0:T(8,128)(2,1)S(1)}, u32[]{:S(2)}, u32[]{:S(2)}) %all-to-all-start) | async-done | bytes 524320 | tf_op jit(solution)/shard_map/all_to_all | solution.py:286
  28.1 0.1 near_sums.1.refs_1_
  28.2 1.3 %collective-permute-start.4 = (bf16[128,128]{1,0:T(8,128)(2,1)S(1)}, bf16[128,128]{1,0:T(8,128)(2,1)S(1)}, u32[]{:S(2)}, u32[]{:S(2)}) collective-permute-start(bf16[128,128]{1,0:T(8,128)(2,1)S(1)} %near_sums.1.refs_1_), channel_id=1, source_target_pairs={{0,24},{8,16},{16,8},{24,0},{1,25},{9,17},{17,9},{25,1},{2,26},{10... | collective-permute-start | bytes 98312 | tf_op jit(solution)/shard_map/ppermute | solution.py:297
  29.5 0.0 collective-permute-start.3
  29.5 4.4 %collective-permute-start.2 = (bf16[128,128]{1,0:T(8,128)(2,1)S(1)}, bf16[128,128]{1,0:T(8,128)(2,1)S(1)}, u32[]{:S(2)}, u32[]{:S(2)}) collective-permute-start(bf16[128,128]{1,0:T(8,128)(2,1)S(1)} %near_sums.1.refs_1_), channel_id=1, source_target_pairs={{0,8},{8,0},{16,24},{24,16},{1,9},{9,1},{17,25},{25,17},{2,10},{10... | collective-permute-start | bytes 98312 | tf_op jit(solution)/shard_map/ppermute | solution.py:297
  33.9 0.0 copy-start.1
  33.9 2.2 %copy-done.1 = bf16[16,8,128,128]{3,2,1,0:T(8,128)(2,1)S(1)} copy-done((bf16[16,8,128,128]{3,2,1,0:T(8,128)(2,1)S(1)}, bf16[16,8,128,128]{3,2,1,0:T(8,128)(2,1)}, u32[]{:S(2)}) %copy-start.1) | copy-done | bytes 4194328
  36.1 0.0 copy-start.2
  36.1 0.1 stacked_weights.1.refs_3_
  36.3 0.0 collective-permute-done.4.refs_4_
  36.3 0.0 collective-permute-done.3.refs_3_
  36.3 0.0 collective-permute-done.2.refs_2_
  36.3 0.2 normed_copies.1
  36.5 14.6 %all_to_all.10.refs_2_ = bf16[16,144,128]{2,1,0:T(8,128)(2,1)S(1)} all-to-all(bf16[16,144,128]{2,1,0:T(8,128)(2,1)S(1)} %normed_copies.1), channel_id=1, replica_groups=mesh['yh'=2,'x'=4,'zh'=4,'zl'=2,'yl'=2,'core'=2] {'yh','x','zl'}, dimensions={0} | all-to-all | bytes 1179648 | tf_op jit(solution)/shard_map/all_to_all | solution.py:304
  51.2 4.3 %collective-permute-start.5 = (f32[4,2,128]{2,1,0:T(2,128)S(1)}, f32[4,2,128]{2,1,0:T(2,128)S(1)}, u32[]{:S(2)}, u32[]{:S(2)}) collective-permute-start(f32[4,2,128]{2,1,0:T(2,128)S(1)} %get-tuple-element.32), channel_id=1, source_target_pairs={{0,1},{1,0},{2,3},{3,2},{4,5},{5,4},{6,7},{7,6},{8,9},{9,8},{10,11... | collective-permute-start | bytes 12296 | tf_op jit(solution)/shard_map/ppermute | solution.py:262
  55.5 0.4 collective-permute-start.7
  55.8 1.1 %collective-permute-start.6 = (f32[4,2,128]{2,1,0:T(2,128)S(1)}, f32[4,2,128]{2,1,0:T(2,128)S(1)}, u32[]{:S(2)}, u32[]{:S(2)}) collective-permute-start(f32[4,2,128]{2,1,0:T(2,128)S(1)} %get-tuple-element.34), channel_id=1, source_target_pairs={{0,2},{1,3},{2,0},{3,1},{4,6},{5,7},{6,4},{7,5},{8,10},{9,11},{10,... | collective-permute-start | bytes 12296 | tf_op jit(solution)/shard_map/ppermute | solution.py:262
  56.9 0.0 copy-done.4
  56.9 0.0 copy-done.2
  56.9 3.3 %residual.1 = bf16[16,8,128,128]{3,2,1,0:T(8,128)(2,1)} custom-call(s32[8,16]{1,0:T(8,128)S(1)} %bitcast.35, bf16[16,8,128,128]{3,2,1,0:T(8,128)(2,1)S(1)} %copy-done.2, bf16[16,144,128]{2,1,0:T(8,128)(2,1)S(1)} %all_to_all.10.refs_2_, bf16[6,256,256]{2,1,0:T(8,128)(2,1)S(1)} %stacked_weights.1.refs_3_), custom_call_target="tpu_custom_call" | custom-call | flops 1073741824 | bytes 8388608 | tf_op jit(solution)/shard_map/residual/pallas_call | solution.py:232
  60.3 0.0 collective-permute-done.5
  60.3 0.0 collective-permute-done.7
  60.3 0.0 collective-permute-done.6
  60.3 0.6 fusion.6
  (6 shorter events, 0.1 us)
Async XLA Ops:
  0.6 20.5 %copy-start = (f32[8,24]{1,0:T(8,128)S(1)}, f32[8,24]{1,0:T(8,128)}, u32[]{:S(2)}) copy-start(f32[8,24]{1,0:T(8,128)} %param.7) | copy-start | bytes 2308
  0.6 20.4 %copy-start.3 = (bf16[8,128,128]{2,1,0:T(8,128)(2,1)S(1)}, bf16[8,128,128]{2,1,0:T(8,128)(2,1)}, u32[]{:S(2)}) copy-start(bf16[8,128,128]{2,1,0:T(8,128)(2,1)} %panels_ref.1) | copy-start | bytes 786436
  0.7 18.7 %collective-permute-start = (bf16[8,128,128]{2,1,0:T(8,128)(2,1)}, bf16[8,128,128]{2,1,0:T(8,128)(2,1)S(1)}, u32[]{:S(2)}, u32[]{:S(2)}) collective-permute-start(bf16[8,128,128]{2,1,0:T(8,128)(2,1)} %panels_ref.1), channel_id=1, source_target_pairs={{0,4},{4,8},{8,12},{12,16},{16,20},{20,24},{24,28},{28,32},{32,36}... | collective-permute-start | bytes 786440 | tf_op jit(solution)/shard_map/ppermute | solution.py:272
  15.8 12.3 %all-to-all-start = ((bf16[16,128,128]{2,1,0:T(8,128)(2,1)}), bf16[16,128,128]{2,1,0:T(8,128)(2,1)S(1)}, u32[]{:S(2)}, u32[]{:S(2)}) async-start(bf16[16,128,128]{2,1,0:T(8,128)(2,1)} %bitcast.37), calls=%async_computation | async-start | bytes 1048576 | tf_op jit(solution)/shard_map/all_to_all | solution.py:286
  19.4 1.6 %collective-permute-start.1 = (bf16[8,128,128]{2,1,0:T(8,128)(2,1)S(1)}, bf16[8,128,128]{2,1,0:T(8,128)(2,1)S(1)}, u32[]{:S(2)}, u32[]{:S(2)}) collective-permute-start(bf16[8,128,128]{2,1,0:T(8,128)(2,1)S(1)} %collective-permute-done), channel_id=1, source_target_pairs={{0,1},{1,0},{2,3},{3,2},{4,5},{5,4},{6,7},{7,6},{8,9},{9,8},{10,11... | collective-permute-start | bytes 786440 | tf_op jit(solution)/shard_map/ppermute | solution.py:273
  22.0 34.9 %copy-start.4 = (s32[16,8]{0,1:T(8,128)S(1)}, s32[16,8]{0,1:T(8,128)}, u32[]{:S(2)}) copy-start(s32[16,8]{0,1:T(8,128)} %param.5) | copy-start | bytes 1540
  28.2 8.1 %collective-permute-start.4 = (bf16[128,128]{1,0:T(8,128)(2,1)S(1)}, bf16[128,128]{1,0:T(8,128)(2,1)S(1)}, u32[]{:S(2)}, u32[]{:S(2)}) collective-permute-start(bf16[128,128]{1,0:T(8,128)(2,1)S(1)} %near_sums.1.refs_1_), channel_id=1, source_target_pairs={{0,24},{8,16},{16,8},{24,0},{1,25},{9,17},{17,9},{25,1},{2,26},{10... | collective-permute-start | bytes 98312 | tf_op jit(solution)/shard_map/ppermute | solution.py:297
  29.5 6.7 %collective-permute-start.3 = (bf16[128,128]{1,0:T(8,128)(2,1)S(1)}, bf16[128,128]{1,0:T(8,128)(2,1)S(1)}, u32[]{:S(2)}, u32[]{:S(2)}) collective-permute-start(bf16[128,128]{1,0:T(8,128)(2,1)S(1)} %near_sums.1.refs_1_), channel_id=1, source_target_pairs={{0,16},{8,24},{16,0},{24,8},{1,17},{9,25},{17,1},{25,9},{2,18},{10... | collective-permute-start | bytes 98312 | tf_op jit(solution)/shard_map/ppermute | solution.py:297
  29.5 6.8 %collective-permute-start.2 = (bf16[128,128]{1,0:T(8,128)(2,1)S(1)}, bf16[128,128]{1,0:T(8,128)(2,1)S(1)}, u32[]{:S(2)}, u32[]{:S(2)}) collective-permute-start(bf16[128,128]{1,0:T(8,128)(2,1)S(1)} %near_sums.1.refs_1_), channel_id=1, source_target_pairs={{0,8},{8,0},{16,24},{24,16},{1,9},{9,1},{17,25},{25,17},{2,10},{10... | collective-permute-start | bytes 98312 | tf_op jit(solution)/shard_map/ppermute | solution.py:297
  33.9 2.2 %copy-start.1 = (bf16[16,8,128,128]{3,2,1,0:T(8,128)(2,1)S(1)}, bf16[16,8,128,128]{3,2,1,0:T(8,128)(2,1)}, u32[]{:S(2)}) copy-start(bf16[16,8,128,128]{3,2,1,0:T(8,128)(2,1)} %refs_1_.3) | copy-start | bytes 12582916
  36.1 20.8 %copy-start.2 = (bf16[16,8,128,128]{3,2,1,0:T(8,128)(2,1)S(1)}, bf16[16,8,128,128]{3,2,1,0:T(8,128)(2,1)}, u32[]{:S(2)}) copy-start(bf16[16,8,128,128]{3,2,1,0:T(8,128)(2,1)} %refs_1_.3) | copy-start | bytes 12582916
  51.2 9.1 %collective-permute-start.5 = (f32[4,2,128]{2,1,0:T(2,128)S(1)}, f32[4,2,128]{2,1,0:T(2,128)S(1)}, u32[]{:S(2)}, u32[]{:S(2)}) collective-permute-start(f32[4,2,128]{2,1,0:T(2,128)S(1)} %get-tuple-element.32), channel_id=1, source_target_pairs={{0,1},{1,0},{2,3},{3,2},{4,5},{5,4},{6,7},{7,6},{8,9},{9,8},{10,11... | collective-permute-start | bytes 12296 | tf_op jit(solution)/shard_map/ppermute | solution.py:262
  55.5 4.8 %collective-permute-start.7 = (f32[4,2,128]{2,1,0:T(2,128)S(1)}, f32[4,2,128]{2,1,0:T(2,128)S(1)}, u32[]{:S(2)}, u32[]{:S(2)}) collective-permute-start(f32[4,2,128]{2,1,0:T(2,128)S(1)} %get-tuple-element.33), channel_id=1, source_target_pairs={{0,3},{1,2},{2,1},{3,0},{4,7},{5,6},{6,5},{7,4},{8,11},{9,10},{10,... | collective-permute-start | bytes 12296 | tf_op jit(solution)/shard_map/ppermute | solution.py:262
  55.8 4.5 %collective-permute-start.6 = (f32[4,2,128]{2,1,0:T(2,128)S(1)}, f32[4,2,128]{2,1,0:T(2,128)S(1)}, u32[]{:S(2)}, u32[]{:S(2)}) collective-permute-start(f32[4,2,128]{2,1,0:T(2,128)S(1)} %get-tuple-element.34), channel_id=1, source_target_pairs={{0,2},{1,3},{2,0},{3,1},{4,6},{5,7},{6,4},{7,5},{8,10},{9,11},{10,... | collective-permute-start | bytes 12296 | tf_op jit(solution)/shard_map/ppermute | solution.py:262

commit v5 on v4

--- a/solution.py
+++ b/solution.py
@@ -255,8 +255,8 @@
     count = blocks.shape[0]
     zero = jnp.uint32(0)
     total = None
-    for step, index in enumerate(indices):
-        starts = (index, *[zero] * (blocks.ndim - 1))
+    for step in (0, 3, 1, 2):
+        starts = (indices[step], *[zero] * (blocks.ndim - 1))
         block = lax.dynamic_slice(blocks, starts, (1, *blocks.shape[1:]))[0]
         if step:
             block = lax.ppermute(block, OCC, [(i, i ^ step) for i in range(count)])
@@ -293,7 +293,7 @@
 
     part, combined = lax.optimization_barrier((near_sums(parts), combined))
     parts = [part]
-    for step in range(1, far):
+    for step in (1, 3, 2):
         parts.append(lax.ppermute(part, "zh", [(i, i ^ step) for i in range(far)]))
     weights = stacked_weights(l3_tiles, combined, panels)
     line = lax.axis_index("zh").reshape(1)

time: 61.1 us -> 60.5 us (level)
    ppermute x3, starting transfers between devices: 5.72 us -> 5.06 us  [occ_sum(): block = lax.ppermute(block, OCC, [(i, i ^ step) for i in range(count)])]
where the time goes in v5:
time: 60.5 us; the launch traced here: 60.3 us
  starting transfers between devices  25.8 us (43%)
  blocking collectives  14.6 us (24%)
  waiting for transfers between devices  7.64 us (13%)
  Pallas kernels  7.6 us (13%)
  local copies, waits for them, and re-layouts  2.27 us (4%)
  between operations  0.84 us (1%)
  matrix products  0.76 us (1%)
  other arithmetic  0.74 us (1%)
    all_to_all x1, blocking collectives, shards(): gathered = lax.all_to_all(copies, NEAR, 0, 0, tiled=True)  14.6 us
    ppermute x1, starting transfers between devices, halo(): mine = lax.ppermute(panels, (*VIR, 'core'), pairs)  11.3 us
    all_to_all x1, waiting for transfers between devices, shards(): lax.all_to_all(partial.reshape(near, -1, width), NEAR, 0, 0, tiled=True)  6.1 us
    ppermute x3, starting transfers between devices, shards(): parts.append(lax.ppermute(part, 'zh', [(i, i ^ step) for i in range(far)]))  5.74 us
    ppermute x3, starting transfers between devices, occ_sum(): block = lax.ppermute(block, OCC, [(i, i ^ step) for i in range(count)])  5.06 us
    pallas_call x1, Pallas kernels, partial_sums(): pl.pallas_call(kernel, in_specs=[pl.BlockSpec(memory_space=pltpu.HBM)] *...  3.83 us
    all_to_all x1, starting transfers between devices, shards(): lax.all_to_all(partial.reshape(near, -1, width), NEAR, 0, 0, tiled=True)  3.59 us
    pallas_call x1, Pallas kernels, residual(): pl.pallas_call(kernel, in_specs=[pl.BlockSpec(memory_space=pltpu.SMEM), *...  3.35 us
  transfers between devices with their start and end apart: 9, of which 2 were waited for; matrix products, arithmetic and copies ran while one was open for 2% of the time, Pallas kernels for 12%

profile of v5, /device:TPU:1, one launch (start us, length us, event | category | flops | bytes accessed | tf_op | source)
XLA Modules:
  0.0 60.3 jit_solution(18108356666432800804)
XLA Ops:
  0.6 0.0 copy-start
  0.6 0.0 copy-start.3
  0.7 11.3 %collective-permute-start = (bf16[8,128,128]{2,1,0:T(8,128)(2,1)}, bf16[8,128,128]{2,1,0:T(8,128)(2,1)S(1)}, u32[]{:S(2)}, u32[]{:S(2)}) collective-permute-start(bf16[8,128,128]{2,1,0:T(8,128)(2,1)} %panels_ref.1), channel_id=1, source_target_pairs={{0,4},{4,8},{8,12},{12,16},{16,20},{20,24},{24,28},{28,32},{32,36}... | collective-permute-start | bytes 786440 | tf_op jit(solution)/shard_map/ppermute | solution.py:272
  12.0 3.8 %partial_sums.1 = bf16[2048,128]{1,0:T(8,128)(2,1)} custom-call(s32[8,16]{1,0:T(8,128)} %bitcast.34, bf16[16,8,128,128]{3,2,1,0:T(8,128)(2,1)} %refs_1_.3, bf16[8,128,128]{2,1,0:T(8,128)(2,1)} %panels_ref.1), custom_call_target="tpu_custom_call" | custom-call | flops 536870912 | bytes 4194304 | tf_op jit(solution)/shard_map/partial_sums/pallas_call | solution.py:77
  15.8 3.6 %all-to-all-start = ((bf16[16,128,128]{2,1,0:T(8,128)(2,1)}), bf16[16,128,128]{2,1,0:T(8,128)(2,1)S(1)}, u32[]{:S(2)}, u32[]{:S(2)}) async-start(bf16[16,128,128]{2,1,0:T(8,128)(2,1)} %bitcast.37), calls=%async_computation | async-start | bytes 1048576 | tf_op jit(solution)/shard_map/all_to_all | solution.py:286
  19.4 0.0 collective-permute-done
  19.4 0.1 collective-permute-start.1
  19.5 1.5 %collective-permute-done.1 = bf16[8,128,128]{2,1,0:T(8,128)(2,1)S(1)} collective-permute-done((bf16[8,128,128]{2,1,0:T(8,128)(2,1)S(1)}, bf16[8,128,128]{2,1,0:T(8,128)(2,1)S(1)}, u32[]{:S(2)}, u32[]{:S(2)}) %collective-permute-start.1) | collective-permute-done | bytes 262176 | tf_op jit(solution)/shard_map/ppermute | solution.py:273
  21.1 0.0 copy-done.3
  21.1 0.1 pad_maximum_fusion
  21.2 0.0 copy-done
  21.2 0.8 %fusion = bf16[1,8,128,128]{3,1,2,0:T(8,128)(2,1)S(1)} fusion(f32[8,24]{1,0:T(8,128)S(1)} %copy-done, bf16[3,8,128,128]{3,2,1,0:T(8,128)(2,1)S(1)} %bitcast.36), kind=kOutput, calls=%fused_computation.1 | convolution fusion | flops 37879808 | bytes 1049344 | tf_op jit(solution)/shard_map/dot_general | solution.py:290
  22.0 0.0 copy-start.4
  22.0 6.1 %all-to-all-done.parts_ref = bf16[16,128,128]{2,1,0:T(8,128)(2,1)S(1)} async-done(((bf16[16,128,128]{2,1,0:T(8,128)(2,1)}), bf16[16,128,128]{2,1,0:T(8,128)(2,1)S(1)}, u32[]{:S(2)}, u32[]{:S(2)}) %all-to-all-start) | async-done | bytes 524320 | tf_op jit(solution)/shard_map/all_to_all | solution.py:286
  28.1 0.1 near_sums.1.refs_1_
  28.2 0.9 %collective-permute-start.4 = (bf16[128,128]{1,0:T(8,128)(2,1)S(1)}, bf16[128,128]{1,0:T(8,128)(2,1)S(1)}, u32[]{:S(2)}, u32[]{:S(2)}) collective-permute-start(bf16[128,128]{1,0:T(8,128)(2,1)S(1)} %near_sums.1.refs_1_), channel_id=1, source_target_pairs={{0,16},{8,24},{16,0},{24,8},{1,17},{9,25},{17,1},{25,9},{2,18},{10... | collective-permute-start | bytes 98312 | tf_op jit(solution)/shard_map/ppermute | solution.py:297
  29.1 0.6 collective-permute-start.3
  29.6 4.3 %collective-permute-start.2 = (bf16[128,128]{1,0:T(8,128)(2,1)S(1)}, bf16[128,128]{1,0:T(8,128)(2,1)S(1)}, u32[]{:S(2)}, u32[]{:S(2)}) collective-permute-start(bf16[128,128]{1,0:T(8,128)(2,1)S(1)} %near_sums.1.refs_1_), channel_id=1, source_target_pairs={{0,8},{8,0},{16,24},{24,16},{1,9},{9,1},{17,25},{25,17},{2,10},{10... | collective-permute-start | bytes 98312 | tf_op jit(solution)/shard_map/ppermute | solution.py:297
  33.9 0.0 copy-start.1
  33.9 2.2 %copy-done.1 = bf16[16,8,128,128]{3,2,1,0:T(8,128)(2,1)S(1)} copy-done((bf16[16,8,128,128]{3,2,1,0:T(8,128)(2,1)S(1)}, bf16[16,8,128,128]{3,2,1,0:T(8,128)(2,1)}, u32[]{:S(2)}) %copy-start.1) | copy-done | bytes 4194328
  36.1 0.0 copy-start.2
  36.1 0.1 stacked_weights.1.refs_3_
  36.3 0.0 collective-permute-done.4.refs_4_
  36.3 0.0 collective-permute-done.3.refs_3_
  36.3 0.0 collective-permute-done.2.refs_2_
  36.3 0.2 normed_copies.1
  36.5 14.6 %all_to_all.10.refs_2_ = bf16[16,144,128]{2,1,0:T(8,128)(2,1)S(1)} all-to-all(bf16[16,144,128]{2,1,0:T(8,128)(2,1)S(1)} %normed_copies.1), channel_id=1, replica_groups=mesh['yh'=2,'x'=4,'zh'=4,'zl'=2,'yl'=2,'core'=2] {'yh','x','zl'}, dimensions={0} | all-to-all | bytes 1179648 | tf_op jit(solution)/shard_map/all_to_all | solution.py:304
  51.2 4.0 %collective-permute-start.5 = (f32[4,2,128]{2,1,0:T(2,128)S(1)}, f32[4,2,128]{2,1,0:T(2,128)S(1)}, u32[]{:S(2)}, u32[]{:S(2)}) collective-permute-start(f32[4,2,128]{2,1,0:T(2,128)S(1)} %get-tuple-element.32), channel_id=1, source_target_pairs={{0,3},{1,2},{2,1},{3,0},{4,7},{5,6},{6,5},{7,4},{8,11},{9,10},{10,... | collective-permute-start | bytes 12296 | tf_op jit(solution)/shard_map/ppermute | solution.py:262
  55.2 1.1 %collective-permute-start.7 = (f32[4,2,128]{2,1,0:T(2,128)S(1)}, f32[4,2,128]{2,1,0:T(2,128)S(1)}, u32[]{:S(2)}, u32[]{:S(2)}) collective-permute-start(f32[4,2,128]{2,1,0:T(2,128)S(1)} %get-tuple-element.33), channel_id=1, source_target_pairs={{0,2},{1,3},{2,0},{3,1},{4,6},{5,7},{6,4},{7,5},{8,10},{9,11},{10,... | collective-permute-start | bytes 12296 | tf_op jit(solution)/shard_map/ppermute | solution.py:262
  56.3 0.0 collective-permute-start.6
  56.3 0.0 copy-done.4
  56.3 0.0 copy-done.2
  56.3 3.3 %residual.1 = bf16[16,8,128,128]{3,2,1,0:T(8,128)(2,1)} custom-call(s32[8,16]{1,0:T(8,128)S(1)} %bitcast.35, bf16[16,8,128,128]{3,2,1,0:T(8,128)(2,1)S(1)} %copy-done.2, bf16[16,144,128]{2,1,0:T(8,128)(2,1)S(1)} %all_to_all.10.refs_2_, bf16[6,256,256]{2,1,0:T(8,128)(2,1)S(1)} %stacked_weights.1.refs_3_), custom_call_target="tpu_custom_call" | custom-call | flops 1073741824 | bytes 8388608 | tf_op jit(solution)/shard_map/residual/pallas_call | solution.py:232
  59.7 0.0 collective-permute-done.5
  59.7 0.0 collective-permute-done.7
  59.7 0.0 collective-permute-done.6
  59.7 0.6 fusion.6
  (6 shorter events, 0.1 us)
Async XLA Ops:
  0.6 20.5 %copy-start = (f32[8,24]{1,0:T(8,128)S(1)}, f32[8,24]{1,0:T(8,128)}, u32[]{:S(2)}) copy-start(f32[8,24]{1,0:T(8,128)} %param.7) | copy-start | bytes 2308
  0.6 20.4 %copy-start.3 = (bf16[8,128,128]{2,1,0:T(8,128)(2,1)S(1)}, bf16[8,128,128]{2,1,0:T(8,128)(2,1)}, u32[]{:S(2)}) copy-start(bf16[8,128,128]{2,1,0:T(8,128)(2,1)} %panels_ref.1) | copy-start | bytes 786436
  0.7 18.7 %collective-permute-start = (bf16[8,128,128]{2,1,0:T(8,128)(2,1)}, bf16[8,128,128]{2,1,0:T(8,128)(2,1)S(1)}, u32[]{:S(2)}, u32[]{:S(2)}) collective-permute-start(bf16[8,128,128]{2,1,0:T(8,128)(2,1)} %panels_ref.1), channel_id=1, source_target_pairs={{0,4},{4,8},{8,12},{12,16},{16,20},{20,24},{24,28},{28,32},{32,36}... | collective-permute-start | bytes 786440 | tf_op jit(solution)/shard_map/ppermute | solution.py:272
  15.8 12.3 %all-to-all-start = ((bf16[16,128,128]{2,1,0:T(8,128)(2,1)}), bf16[16,128,128]{2,1,0:T(8,128)(2,1)S(1)}, u32[]{:S(2)}, u32[]{:S(2)}) async-start(bf16[16,128,128]{2,1,0:T(8,128)(2,1)} %bitcast.37), calls=%async_computation | async-start | bytes 1048576 | tf_op jit(solution)/shard_map/all_to_all | solution.py:286
  19.4 1.6 %collective-permute-start.1 = (bf16[8,128,128]{2,1,0:T(8,128)(2,1)S(1)}, bf16[8,128,128]{2,1,0:T(8,128)(2,1)S(1)}, u32[]{:S(2)}, u32[]{:S(2)}) collective-permute-start(bf16[8,128,128]{2,1,0:T(8,128)(2,1)S(1)} %collective-permute-done), channel_id=1, source_target_pairs={{0,1},{1,0},{2,3},{3,2},{4,5},{5,4},{6,7},{7,6},{8,9},{9,8},{10,11... | collective-permute-start | bytes 786440 | tf_op jit(solution)/shard_map/ppermute | solution.py:273
  22.0 34.3 %copy-start.4 = (s32[16,8]{0,1:T(8,128)S(1)}, s32[16,8]{0,1:T(8,128)}, u32[]{:S(2)}) copy-start(s32[16,8]{0,1:T(8,128)} %param.5) | copy-start | bytes 1540
  28.2 8.1 %collective-permute-start.4 = (bf16[128,128]{1,0:T(8,128)(2,1)S(1)}, bf16[128,128]{1,0:T(8,128)(2,1)S(1)}, u32[]{:S(2)}, u32[]{:S(2)}) collective-permute-start(bf16[128,128]{1,0:T(8,128)(2,1)S(1)} %near_sums.1.refs_1_), channel_id=1, source_target_pairs={{0,16},{8,24},{16,0},{24,8},{1,17},{9,25},{17,1},{25,9},{2,18},{10... | collective-permute-start | bytes 98312 | tf_op jit(solution)/shard_map/ppermute | solution.py:297
  29.1 7.2 %collective-permute-start.3 = (bf16[128,128]{1,0:T(8,128)(2,1)S(1)}, bf16[128,128]{1,0:T(8,128)(2,1)S(1)}, u32[]{:S(2)}, u32[]{:S(2)}) collective-permute-start(bf16[128,128]{1,0:T(8,128)(2,1)S(1)} %near_sums.1.refs_1_), channel_id=1, source_target_pairs={{0,24},{8,16},{16,8},{24,0},{1,25},{9,17},{17,9},{25,1},{2,26},{10... | collective-permute-start | bytes 98312 | tf_op jit(solution)/shard_map/ppermute | solution.py:297
  29.6 6.7 %collective-permute-start.2 = (bf16[128,128]{1,0:T(8,128)(2,1)S(1)}, bf16[128,128]{1,0:T(8,128)(2,1)S(1)}, u32[]{:S(2)}, u32[]{:S(2)}) collective-permute-start(bf16[128,128]{1,0:T(8,128)(2,1)S(1)} %near_sums.1.refs_1_), channel_id=1, source_target_pairs={{0,8},{8,0},{16,24},{24,16},{1,9},{9,1},{17,25},{25,17},{2,10},{10... | collective-permute-start | bytes 98312 | tf_op jit(solution)/shard_map/ppermute | solution.py:297
  33.9 2.2 %copy-start.1 = (bf16[16,8,128,128]{3,2,1,0:T(8,128)(2,1)S(1)}, bf16[16,8,128,128]{3,2,1,0:T(8,128)(2,1)}, u32[]{:S(2)}) copy-start(bf16[16,8,128,128]{3,2,1,0:T(8,128)(2,1)} %refs_1_.3) | copy-start | bytes 12582916
  36.1 20.2 %copy-start.2 = (bf16[16,8,128,128]{3,2,1,0:T(8,128)(2,1)S(1)}, bf16[16,8,128,128]{3,2,1,0:T(8,128)(2,1)}, u32[]{:S(2)}) copy-start(bf16[16,8,128,128]{3,2,1,0:T(8,128)(2,1)} %refs_1_.3) | copy-start | bytes 12582916
  51.2 8.4 %collective-permute-start.5 = (f32[4,2,128]{2,1,0:T(2,128)S(1)}, f32[4,2,128]{2,1,0:T(2,128)S(1)}, u32[]{:S(2)}, u32[]{:S(2)}) collective-permute-start(f32[4,2,128]{2,1,0:T(2,128)S(1)} %get-tuple-element.32), channel_id=1, source_target_pairs={{0,3},{1,2},{2,1},{3,0},{4,7},{5,6},{6,5},{7,4},{8,11},{9,10},{10,... | collective-permute-start | bytes 12296 | tf_op jit(solution)/shard_map/ppermute | solution.py:262
  55.2 4.4 %collective-permute-start.7 = (f32[4,2,128]{2,1,0:T(2,128)S(1)}, f32[4,2,128]{2,1,0:T(2,128)S(1)}, u32[]{:S(2)}, u32[]{:S(2)}) collective-permute-start(f32[4,2,128]{2,1,0:T(2,128)S(1)} %get-tuple-element.33), channel_id=1, source_target_pairs={{0,2},{1,3},{2,0},{3,1},{4,6},{5,7},{6,4},{7,5},{8,10},{9,11},{10,... | collective-permute-start | bytes 12296 | tf_op jit(solution)/shard_map/ppermute | solution.py:262
  56.3 3.4 %collective-permute-start.6 = (f32[4,2,128]{2,1,0:T(2,128)S(1)}, f32[4,2,128]{2,1,0:T(2,128)S(1)}, u32[]{:S(2)}, u32[]{:S(2)}) collective-permute-start(f32[4,2,128]{2,1,0:T(2,128)S(1)} %get-tuple-element.34), channel_id=1, source_target_pairs={{0,1},{1,0},{2,3},{3,2},{4,5},{5,4},{6,7},{7,6},{8,9},{9,8},{10,11... | collective-permute-start | bytes 12296 | tf_op jit(solution)/shard_map/ppermute | solution.py:262

commit v6 on v5

--- a/solution.py
+++ b/solution.py
@@ -190,15 +190,20 @@
     )(l3, combined, panels)
 
 
-def final_kernel(flags_ref, l3_ref, normed_ref, weights_ref, r3_ref, out_ref, sems, *, block):
+def final_kernel(
+    core_ref, flags_ref, l3_ref, normed_ref, weights_ref, r3_ref, out_ref, flags, sem, sems, *, block
+):
     triples, pairs, width, _ = l3_ref.shape
     held = triples // normed_ref.shape[0]
+    fetch = pltpu.make_async_copy(flags_ref, flags, sem)
+    fetch.start()
     stores = [pltpu.make_async_copy(out_ref.at[t], r3_ref.at[t], sems.at[t]) for t in range(triples)]
 
     def product(lhs, index):
         lhs = jnp.concatenate([jnp.concatenate(row, axis=1) for row in lhs], axis=0)
         return jnp.dot(lhs, weights_ref[index], preferred_element_type=jnp.float32)
 
+    fetch.wait()
     for first in range(0, triples, block):
         here = range(first, first + block)
         normed = [normed_ref[t // held, t % held * width : (t % held + 1) * width] for t in here]
@@ -214,7 +219,7 @@
             ]
             for t in here:
                 for j in range(4):
-                    mask = flags_ref[p + j, t].astype(jnp.float32)
+                    mask = flags[p + j, t].astype(jnp.float32)
                     tile = sums[j][(t - first) * width : (t - first + 1) * width] * mask
                     out_ref[t, p + j] = tile.astype(jnp.bfloat16)
         for t in here:
@@ -223,19 +228,32 @@
         store.wait()
 
 
-def residual(flags, l3, normed, weights, block=2):
+def residual(turn, core, flags, l3, normed, weights, before=None, block=2):
     triples, pairs, width, _ = l3.shape
 
-    def kernel(*refs):
-        final_kernel(*refs, block=block)
-
+    def kernel(core_ref, *refs):
+        refs = refs[:4] + refs[5:] if before is not None else refs
+
+        @pl.when(core_ref[0] == turn)
+        def _():
+            final_kernel(core_ref, *refs, block=block)
+
+    hbm = pl.BlockSpec(memory_space=pltpu.HBM)
+    operands = [core, flags, l3, normed, weights]
+    in_specs = [pl.BlockSpec(memory_space=pltpu.SMEM), hbm, *whole(3)]
+    if before is not None:
+        operands.append(before)
+        in_specs.append(hbm)
     return pl.pallas_call(
         kernel,
-        in_specs=[pl.BlockSpec(memory_space=pltpu.SMEM), *whole(3)],
-        out_specs=pl.BlockSpec(memory_space=pltpu.HBM),
+        in_specs=in_specs,
+        out_specs=hbm,
         out_shape=jax.ShapeDtypeStruct(l3.shape, jnp.bfloat16),
+        input_output_aliases={} if before is None else {5: 0},
         scratch_shapes=[
             pltpu.VMEM(l3.shape, jnp.bfloat16),
+            pltpu.SMEM(flags.shape, jnp.int32),
+            pltpu.SemaphoreType.DMA,
             pltpu.SemaphoreType.DMA((triples,)),
         ],
         compiler_params=params(MEDIUM),
@@ -243,7 +261,7 @@
             flops=4 * triples * pairs * width**3, bytes_accessed=l3.size * 4, transcendentals=0
         ),
         name="residual",
-    )(flags, l3, normed, weights)
+    )(*operands)
 
 
 def own_indices():
@@ -255,7 +273,7 @@
     count = blocks.shape[0]
     zero = jnp.uint32(0)
     total = None
-    for step in (0, 3, 1, 2):
+    for step in (0, 3, 2, 1):
         starts = (indices[step], *[zero] * (blocks.ndim - 1))
         block = lax.dynamic_slice(blocks, starts, (1, *blocks.shape[1:]))[0]
         if step:
@@ -293,20 +311,25 @@
 
     part, combined = lax.optimization_barrier((near_sums(parts), combined))
     parts = [part]
-    for step in (1, 3, 2):
+    for step in (2, 3, 1):
         parts.append(lax.ppermute(part, "zh", [(i, i ^ step) for i in range(far)]))
     weights = stacked_weights(l3_tiles, combined, panels)
     line = lax.axis_index("zh").reshape(1)
+    core = lax.axis_index("core").reshape(1)
     indices = own_indices()
-    parts, weights, line, indices = lax.optimization_barrier((parts, weights, line, indices))
+    parts, weights, line, core, indices = lax.optimization_barrier(
+        (parts, weights, line, core, indices)
+    )
 
     copies = normed_copies(parts, line, rows, near)
     gathered = lax.all_to_all(copies, NEAR, 0, 0, tiled=True)
     high_low = gathered[:, -EXTRA:][:, : 2 * triples // near * rows].astype(jnp.float32)
     high_low = high_low.reshape(near, 2, triples // near, rows, width)
     local = (high_low[:, 0] + high_low[:, 1]).reshape(occ_count, triples // occ_count, rows, width)
+    r3_tiles = residual(1, core, flags, l3_tiles, gathered, weights)
+    local, r3_tiles = lax.optimization_barrier((local, r3_tiles))
     total = occ_sum(local, indices)
-    r3_tiles = residual(flags, l3_tiles, gathered, weights)
+    r3_tiles = residual(0, core, flags, l3_tiles, gathered, weights, r3_tiles)
     l2_block = (total / jnp.sqrt(jnp.float32(pairs * vir_count))).astype(jnp.bfloat16)
     return (r3_tiles, l2_block)
 

time: 60.5 us -> 60.2 us (level)
  the two profiles are of different devices: /device:TPU:1 before, /device:TPU:64 now
where the time goes in v6:
time: 60.2 us; the launch traced here: 59.9 us
  starting transfers between devices  21.1 us (35%)
  blocking collectives  17.4 us (29%)
  waiting for transfers between devices  8.99 us (15%)
  Pallas kernels  7.77 us (13%)
  local copies, waits for them, and re-layouts  2.27 us (4%)
  between operations  0.84 us (1%)
  matrix products  0.76 us (1%)
  other arithmetic  0.74 us (1%)
    all_to_all x1, blocking collectives, shards(): gathered = lax.all_to_all(copies, NEAR, 0, 0, tiled=True)  17.4 us
    all_to_all x1, starting transfers between devices, shards(): lax.all_to_all(partial.reshape(near, -1, width), NEAR, 0, 0, tiled=True)  9.61 us
    all_to_all x1, waiting for transfers between devices, shards(): lax.all_to_all(partial.reshape(near, -1, width), NEAR, 0, 0, tiled=True)  6.78 us
    ppermute x3, starting transfers between devices, shards(): parts.append(lax.ppermute(part, 'zh', [(i, i ^ step) for i in range(far)]))  6.58 us
    pallas_call x1, Pallas kernels, partial_sums(): pl.pallas_call(kernel, in_specs=[pl.BlockSpec(memory_space=pltpu.HBM)] *...  3.83 us
    pallas_call x2, Pallas kernels, residual(): pl.pallas_call(kernel, in_specs=in_specs, out_specs=hbm, out_shape=jax.Sh...  3.51 us
    ppermute x3, starting transfers between devices, occ_sum(): block = lax.ppermute(block, OCC, [(i, i ^ step) for i in range(count)])  2.83 us
    unnamed x11, local copies, waits for them, and re-layouts  2.25 us
  transfers between devices with their start and end apart: 9, of which 3 were waited for; matrix products, arithmetic and copies ran while one was open for 2% of the time, Pallas kernels for 12%

profile of v6, /device:TPU:64, one launch (start us, length us, event | category | flops | bytes accessed | tf_op | source)
XLA Modules:
  0.0 59.9 jit_solution(11523011611223732983)
XLA Ops:
  0.6 0.0 copy-start
  0.6 0.0 copy-start.3
  0.7 2.0 %collective-permute-start = (bf16[8,128,128]{2,1,0:T(8,128)(2,1)}, bf16[8,128,128]{2,1,0:T(8,128)(2,1)S(1)}, u32[]{:S(2)}, u32[]{:S(2)}) collective-permute-start(bf16[8,128,128]{2,1,0:T(8,128)(2,1)} %panels_ref.1), channel_id=1, source_target_pairs={{0,4},{4,8},{8,12},{12,16},{16,20},{20,24},{24,28},{28,32},{32,36}... | collective-permute-start | bytes 786440 | tf_op jit(solution)/shard_map/ppermute | solution.py:290
  2.6 3.8 %partial_sums.1 = bf16[2048,128]{1,0:T(8,128)(2,1)} custom-call(s32[8,16]{1,0:T(8,128)} %bitcast.35, bf16[16,8,128,128]{3,2,1,0:T(8,128)(2,1)} %refs_1_.5, bf16[8,128,128]{2,1,0:T(8,128)(2,1)} %panels_ref.1), custom_call_target="tpu_custom_call" | custom-call | flops 536870912 | bytes 4194304 | tf_op jit(solution)/shard_map/partial_sums/pallas_call | solution.py:77
  6.5 9.6 %all-to-all-start = ((bf16[16,128,128]{2,1,0:T(8,128)(2,1)}), bf16[16,128,128]{2,1,0:T(8,128)(2,1)S(1)}, u32[]{:S(2)}, u32[]{:S(2)}) async-start(bf16[16,128,128]{2,1,0:T(8,128)(2,1)} %bitcast.39), calls=%async_computation | async-start | bytes 1048576 | tf_op jit(solution)/shard_map/all_to_all | solution.py:304
  16.1 0.0 collective-permute-done
  16.1 0.1 collective-permute-start.1
  16.2 1.5 %collective-permute-done.1 = bf16[8,128,128]{2,1,0:T(8,128)(2,1)S(1)} collective-permute-done((bf16[8,128,128]{2,1,0:T(8,128)(2,1)S(1)}, bf16[8,128,128]{2,1,0:T(8,128)(2,1)S(1)}, u32[]{:S(2)}, u32[]{:S(2)}) %collective-permute-start.1) | collective-permute-done | bytes 262176 | tf_op jit(solution)/shard_map/ppermute | solution.py:291
  17.8 0.0 copy-done.3
  17.8 0.1 pad_maximum_fusion
  17.9 0.0 copy-done
  17.9 0.8 %fusion = bf16[1,8,128,128]{3,1,2,0:T(8,128)(2,1)S(1)} fusion(f32[8,24]{1,0:T(8,128)S(1)} %copy-done, bf16[3,8,128,128]{3,2,1,0:T(8,128)(2,1)S(1)} %bitcast.38), kind=kOutput, calls=%fused_computation.1 | convolution fusion | flops 37879808 | bytes 1049344 | tf_op jit(solution)/shard_map/dot_general | solution.py:308
  18.7 0.0 copy-start.4
  18.7 6.8 %all-to-all-done.parts_ref = bf16[16,128,128]{2,1,0:T(8,128)(2,1)S(1)} async-done(((bf16[16,128,128]{2,1,0:T(8,128)(2,1)}), bf16[16,128,128]{2,1,0:T(8,128)(2,1)S(1)}, u32[]{:S(2)}, u32[]{:S(2)}) %all-to-all-start) | async-done | bytes 524320 | tf_op jit(solution)/shard_map/all_to_all | solution.py:304
  25.5 0.1 near_sums.1.refs_1_
  25.6 3.6 %collective-permute-start.2 = (bf16[128,128]{1,0:T(8,128)(2,1)S(1)}, bf16[128,128]{1,0:T(8,128)(2,1)S(1)}, u32[]{:S(2)}, u32[]{:S(2)}) collective-permute-start(bf16[128,128]{1,0:T(8,128)(2,1)S(1)} %near_sums.1.refs_1_), channel_id=1, source_target_pairs={{0,16},{8,24},{16,0},{24,8},{1,17},{9,25},{17,1},{25,9},{2,18},{10... | collective-permute-start | bytes 98312 | tf_op jit(solution)/shard_map/ppermute | solution.py:315
  29.1 0.0 collective-permute-start.3
  29.1 3.0 %collective-permute-start.4 = (bf16[128,128]{1,0:T(8,128)(2,1)S(1)}, bf16[128,128]{1,0:T(8,128)(2,1)S(1)}, u32[]{:S(2)}, u32[]{:S(2)}) collective-permute-start(bf16[128,128]{1,0:T(8,128)(2,1)S(1)} %near_sums.1.refs_1_), channel_id=1, source_target_pairs={{0,8},{8,0},{16,24},{24,16},{1,9},{9,1},{17,25},{25,17},{2,10},{10... | collective-permute-start | bytes 98312 | tf_op jit(solution)/shard_map/ppermute | solution.py:315
  32.2 0.0 copy-start.1
  32.2 2.2 %copy-done.1 = bf16[16,8,128,128]{3,2,1,0:T(8,128)(2,1)S(1)} copy-done((bf16[16,8,128,128]{3,2,1,0:T(8,128)(2,1)S(1)}, bf16[16,8,128,128]{3,2,1,0:T(8,128)(2,1)}, u32[]{:S(2)}) %copy-start.1) | copy-done | bytes 4194328
  34.3 0.0 copy-start.2
  34.3 0.1 stacked_weights.1.refs_3_
  34.5 0.0 collective-permute-done.2.refs_2_
  34.5 0.7 %collective-permute-done.3.refs_3_ = bf16[128,128]{1,0:T(8,128)(2,1)S(1)} collective-permute-done((bf16[128,128]{1,0:T(8,128)(2,1)S(1)}, bf16[128,128]{1,0:T(8,128)(2,1)S(1)}, u32[]{:S(2)}, u32[]{:S(2)}) %collective-permute-start.3) | collective-permute-done | bytes 32800 | tf_op jit(solution)/shard_map/ppermute | solution.py:315
  35.2 0.0 collective-permute-done.4.refs_4_
  35.2 0.2 normed_copies.1
  35.4 17.4 %all_to_all.10.refs_2_ = bf16[16,144,128]{2,1,0:T(8,128)(2,1)S(1)} all-to-all(bf16[16,144,128]{2,1,0:T(8,128)(2,1)S(1)} %normed_copies.1), channel_id=1, replica_groups=mesh['yh'=2,'x'=4,'zh'=4,'zl'=2,'yl'=2,'core'=2] {'yh','x','zl'}, dimensions={0} | all-to-all | bytes 1179648 | tf_op jit(solution)/shard_map/all_to_all | solution.py:325
  52.9 0.0 copy-done.4
  52.9 0.0 copy-done.2
  52.9 0.2 residual.2.refs_4_
  53.1 1.5 %collective-permute-start.5 = (f32[4,2,128]{2,1,0:T(2,128)S(1)}, f32[4,2,128]{2,1,0:T(2,128)S(1)}, u32[]{:S(2)}, u32[]{:S(2)}) collective-permute-start(f32[4,2,128]{2,1,0:T(2,128)S(1)} %get-tuple-element.38), channel_id=1, source_target_pairs={{0,3},{1,2},{2,1},{3,0},{4,7},{5,6},{6,5},{7,4},{8,11},{9,10},{10,... | collective-permute-start | bytes 12296 | tf_op jit(solution)/shard_map/ppermute | solution.py:280
  54.6 1.3 %collective-permute-start.6 = (f32[4,2,128]{2,1,0:T(2,128)S(1)}, f32[4,2,128]{2,1,0:T(2,128)S(1)}, u32[]{:S(2)}, u32[]{:S(2)}) collective-permute-start(f32[4,2,128]{2,1,0:T(2,128)S(1)} %get-tuple-element.40), channel_id=1, source_target_pairs={{0,2},{1,3},{2,0},{3,1},{4,6},{5,7},{6,4},{7,5},{8,10},{9,11},{10,... | collective-permute-start | bytes 12296 | tf_op jit(solution)/shard_map/ppermute | solution.py:280
  55.9 0.0 collective-permute-start.7
  55.9 3.4 %residual.3 = bf16[16,8,128,128]{3,2,1,0:T(8,128)(2,1)} custom-call(s32[1]{0:T(128)} %bitcast.4.core_ref, s32[8,16]{1,0:T(8,128)S(1)} %bitcast.37, bf16[16,8,128,128]{3,2,1,0:T(8,128)(2,1)S(1)} %copy-done.2, bf16[16,144,128]{2,1,0:T(8,128)(2,1)S(1)} %all_to_all.10.refs_2_, ...), custom_call_target="tpu_custom_call", output_to_operand_aliasing={{}: (5, {})} | custom-call | flops 1073741824 | bytes 8388608 | tf_op jit(solution)/shard_map/residual/pallas_call | solution.py:247
  59.3 0.0 collective-permute-done.5
  59.3 0.0 collective-permute-done.6
  59.3 0.0 collective-permute-done.7
  59.3 0.6 fusion.6
  (6 shorter events, 0.1 us)
Async XLA Ops:
  0.6 17.3 %copy-start = (f32[8,24]{1,0:T(8,128)S(1)}, f32[8,24]{1,0:T(8,128)}, u32[]{:S(2)}) copy-start(f32[8,24]{1,0:T(8,128)} %param.7) | copy-start | bytes 2308
  0.6 17.1 %copy-start.3 = (bf16[8,128,128]{2,1,0:T(8,128)(2,1)S(1)}, bf16[8,128,128]{2,1,0:T(8,128)(2,1)}, u32[]{:S(2)}) copy-start(bf16[8,128,128]{2,1,0:T(8,128)(2,1)} %panels_ref.1) | copy-start | bytes 786436
  0.7 15.5 %collective-permute-start = (bf16[8,128,128]{2,1,0:T(8,128)(2,1)}, bf16[8,128,128]{2,1,0:T(8,128)(2,1)S(1)}, u32[]{:S(2)}, u32[]{:S(2)}) collective-permute-start(bf16[8,128,128]{2,1,0:T(8,128)(2,1)} %panels_ref.1), channel_id=1, source_target_pairs={{0,4},{4,8},{8,12},{12,16},{16,20},{20,24},{24,28},{28,32},{32,36}... | collective-permute-start | bytes 786440 | tf_op jit(solution)/shard_map/ppermute | solution.py:290
  6.5 19.0 %all-to-all-start = ((bf16[16,128,128]{2,1,0:T(8,128)(2,1)}), bf16[16,128,128]{2,1,0:T(8,128)(2,1)S(1)}, u32[]{:S(2)}, u32[]{:S(2)}) async-start(bf16[16,128,128]{2,1,0:T(8,128)(2,1)} %bitcast.39), calls=%async_computation | async-start | bytes 1048576 | tf_op jit(solution)/shard_map/all_to_all | solution.py:304
  16.1 1.6 %collective-permute-start.1 = (bf16[8,128,128]{2,1,0:T(8,128)(2,1)S(1)}, bf16[8,128,128]{2,1,0:T(8,128)(2,1)S(1)}, u32[]{:S(2)}, u32[]{:S(2)}) collective-permute-start(bf16[8,128,128]{2,1,0:T(8,128)(2,1)S(1)} %collective-permute-done), channel_id=1, source_target_pairs={{0,1},{1,0},{2,3},{3,2},{4,5},{5,4},{6,7},{7,6},{8,9},{9,8},{10,11... | collective-permute-start | bytes 786440 | tf_op jit(solution)/shard_map/ppermute | solution.py:291
  18.7 34.2 %copy-start.4 = (s32[16,8]{0,1:T(8,128)S(1)}, s32[16,8]{0,1:T(8,128)}, u32[]{:S(2)}) copy-start(s32[16,8]{0,1:T(8,128)} %param.5) | copy-start | bytes 1540
  25.6 8.9 %collective-permute-start.2 = (bf16[128,128]{1,0:T(8,128)(2,1)S(1)}, bf16[128,128]{1,0:T(8,128)(2,1)S(1)}, u32[]{:S(2)}, u32[]{:S(2)}) collective-permute-start(bf16[128,128]{1,0:T(8,128)(2,1)S(1)} %near_sums.1.refs_1_), channel_id=1, source_target_pairs={{0,16},{8,24},{16,0},{24,8},{1,17},{9,25},{17,1},{25,9},{2,18},{10... | collective-permute-start | bytes 98312 | tf_op jit(solution)/shard_map/ppermute | solution.py:315
  29.1 6.0 %collective-permute-start.3 = (bf16[128,128]{1,0:T(8,128)(2,1)S(1)}, bf16[128,128]{1,0:T(8,128)(2,1)S(1)}, u32[]{:S(2)}, u32[]{:S(2)}) collective-permute-start(bf16[128,128]{1,0:T(8,128)(2,1)S(1)} %near_sums.1.refs_1_), channel_id=1, source_target_pairs={{0,24},{8,16},{16,8},{24,0},{1,25},{9,17},{17,9},{25,1},{2,26},{10... | collective-permute-start | bytes 98312 | tf_op jit(solution)/shard_map/ppermute | solution.py:315
  29.1 6.0 %collective-permute-start.4 = (bf16[128,128]{1,0:T(8,128)(2,1)S(1)}, bf16[128,128]{1,0:T(8,128)(2,1)S(1)}, u32[]{:S(2)}, u32[]{:S(2)}) collective-permute-start(bf16[128,128]{1,0:T(8,128)(2,1)S(1)} %near_sums.1.refs_1_), channel_id=1, source_target_pairs={{0,8},{8,0},{16,24},{24,16},{1,9},{9,1},{17,25},{25,17},{2,10},{10... | collective-permute-start | bytes 98312 | tf_op jit(solution)/shard_map/ppermute | solution.py:315
  32.2 2.2 %copy-start.1 = (bf16[16,8,128,128]{3,2,1,0:T(8,128)(2,1)S(1)}, bf16[16,8,128,128]{3,2,1,0:T(8,128)(2,1)}, u32[]{:S(2)}) copy-start(bf16[16,8,128,128]{3,2,1,0:T(8,128)(2,1)} %refs_1_.5) | copy-start | bytes 12582916
  34.3 18.6 %copy-start.2 = (bf16[16,8,128,128]{3,2,1,0:T(8,128)(2,1)S(1)}, bf16[16,8,128,128]{3,2,1,0:T(8,128)(2,1)}, u32[]{:S(2)}) copy-start(bf16[16,8,128,128]{3,2,1,0:T(8,128)(2,1)} %refs_1_.5) | copy-start | bytes 12582916
  53.1 6.2 %collective-permute-start.5 = (f32[4,2,128]{2,1,0:T(2,128)S(1)}, f32[4,2,128]{2,1,0:T(2,128)S(1)}, u32[]{:S(2)}, u32[]{:S(2)}) collective-permute-start(f32[4,2,128]{2,1,0:T(2,128)S(1)} %get-tuple-element.38), channel_id=1, source_target_pairs={{0,3},{1,2},{2,1},{3,0},{4,7},{5,6},{6,5},{7,4},{8,11},{9,10},{10,... | collective-permute-start | bytes 12296 | tf_op jit(solution)/shard_map/ppermute | solution.py:280
  54.6 4.7 %collective-permute-start.6 = (f32[4,2,128]{2,1,0:T(2,128)S(1)}, f32[4,2,128]{2,1,0:T(2,128)S(1)}, u32[]{:S(2)}, u32[]{:S(2)}) collective-permute-start(f32[4,2,128]{2,1,0:T(2,128)S(1)} %get-tuple-element.40), channel_id=1, source_target_pairs={{0,2},{1,3},{2,0},{3,1},{4,6},{5,7},{6,4},{7,5},{8,10},{9,11},{10,... | collective-permute-start | bytes 12296 | tf_op jit(solution)/shard_map/ppermute | solution.py:280
  55.9 3.4 %collective-permute-start.7 = (f32[4,2,128]{2,1,0:T(2,128)S(1)}, f32[4,2,128]{2,1,0:T(2,128)S(1)}, u32[]{:S(2)}, u32[]{:S(2)}) collective-permute-start(f32[4,2,128]{2,1,0:T(2,128)S(1)} %get-tuple-element.39), channel_id=1, source_target_pairs={{0,1},{1,0},{2,3},{3,2},{4,5},{5,4},{6,7},{7,6},{8,9},{9,8},{10,11... | collective-permute-start | bytes 12296 | tf_op jit(solution)/shard_map/ppermute | solution.py:280

commit v7 on v6

--- a/solution.py
+++ b/solution.py
@@ -203,14 +203,16 @@
         lhs = jnp.concatenate([jnp.concatenate(row, axis=1) for row in lhs], axis=0)
         return jnp.dot(lhs, weights_ref[index], preferred_element_type=jnp.float32)
 
-    fetch.wait()
-    for first in range(0, triples, block):
-        here = range(first, first + block)
+    edges = [0, 1, *range(2, triples - 1, block), triples - 1, triples]
+    for first, after in zip(edges, edges[1:]):
+        here = range(first, after)
         normed = [normed_ref[t // held, t % held * width : (t % held + 1) * width] for t in here]
         for k, p in enumerate(range(0, pairs, 4)):
             one = product([[l3_ref[t, p], normed[t - first]] for t in here], 3 * k)
             two = product([[l3_ref[t, p + 2], normed[t - first]] for t in here], 3 * k + 1)
             direct = product([[l3_ref[t, p + 1], l3_ref[t, p + 3]] for t in here], 3 * k + 2)
+            if first == 0 and k == 0:
+                fetch.wait()
             sums = [
                 one[:, :width],
                 one[:, width:] + direct[:, :width],
@@ -273,7 +275,7 @@
     count = blocks.shape[0]
     zero = jnp.uint32(0)
     total = None
-    for step in (0, 3, 2, 1):
+    for step in (0, 2, 3, 1):
         starts = (indices[step], *[zero] * (blocks.ndim - 1))
         block = lax.dynamic_slice(blocks, starts, (1, *blocks.shape[1:]))[0]
         if step:

time: 60.2 us -> 59.8 us (level)
  the two profiles are of different devices: /device:TPU:64 before, /device:TPU:1 now
where the time goes in v7:
time: 59.8 us; the launch traced here: 58.9 us
  starting transfers between devices  22.9 us (38%)
  blocking collectives  14.6 us (24%)
  waiting for transfers between devices  9.05 us (15%)
  Pallas kernels  7.73 us (13%)
  local copies, waits for them, and re-layouts  2.27 us (4%)
  between operations  0.84 us (1%)
  matrix products  0.76 us (1%)
  other arithmetic  0.74 us (1%)
    all_to_all x1, blocking collectives, shards(): gathered = lax.all_to_all(copies, NEAR, 0, 0, tiled=True)  14.6 us
    ppermute x1, starting transfers between devices, halo(): mine = lax.ppermute(panels, (*VIR, 'core'), pairs)  11.3 us
    all_to_all x1, waiting for transfers between devices, shards(): lax.all_to_all(partial.reshape(near, -1, width), NEAR, 0, 0, tiled=True)  6.1 us
    ppermute x3, starting transfers between devices, shards(): parts.append(lax.ppermute(part, 'zh', [(i, i ^ step) for i in range(far)]))  5.74 us
    pallas_call x1, Pallas kernels, partial_sums(): pl.pallas_call(kernel, in_specs=[pl.BlockSpec(memory_space=pltpu.HBM)] *...  3.83 us
    all_to_all x1, starting transfers between devices, shards(): lax.all_to_all(partial.reshape(near, -1, width), NEAR, 0, 0, tiled=True)  3.59 us
    pallas_call x2, Pallas kernels, residual(): pl.pallas_call(kernel, in_specs=in_specs, out_specs=hbm, out_shape=jax.Sh...  3.47 us
    unnamed x11, local copies, waits for them, and re-layouts  2.25 us
  transfers between devices with their start and end apart: 9, of which 4 were waited for; matrix products, arithmetic and copies ran while one was open for 2% of the time, Pallas kernels for 7%

profile of v7, /device:TPU:1, one launch (start us, length us, event | category | flops | bytes accessed | tf_op | source)
XLA Modules:
  0.0 58.9 jit_solution(556366847030187194)
XLA Ops:
  0.6 0.0 copy-start
  0.6 0.0 copy-start.3
  0.7 11.3 %collective-permute-start = (bf16[8,128,128]{2,1,0:T(8,128)(2,1)}, bf16[8,128,128]{2,1,0:T(8,128)(2,1)S(1)}, u32[]{:S(2)}, u32[]{:S(2)}) collective-permute-start(bf16[8,128,128]{2,1,0:T(8,128)(2,1)} %panels_ref.1), channel_id=1, source_target_pairs={{0,4},{4,8},{8,12},{12,16},{16,20},{20,24},{24,28},{28,32},{32,36}... | collective-permute-start | bytes 786440 | tf_op jit(solution)/shard_map/ppermute | solution.py:292
  12.0 3.8 %partial_sums.1 = bf16[2048,128]{1,0:T(8,128)(2,1)} custom-call(s32[8,16]{1,0:T(8,128)} %bitcast.35, bf16[16,8,128,128]{3,2,1,0:T(8,128)(2,1)} %refs_1_.5, bf16[8,128,128]{2,1,0:T(8,128)(2,1)} %panels_ref.1), custom_call_target="tpu_custom_call" | custom-call | flops 536870912 | bytes 4194304 | tf_op jit(solution)/shard_map/partial_sums/pallas_call | solution.py:77
  15.8 3.6 %all-to-all-start = ((bf16[16,128,128]{2,1,0:T(8,128)(2,1)}), bf16[16,128,128]{2,1,0:T(8,128)(2,1)S(1)}, u32[]{:S(2)}, u32[]{:S(2)}) async-start(bf16[16,128,128]{2,1,0:T(8,128)(2,1)} %bitcast.39), calls=%async_computation | async-start | bytes 1048576 | tf_op jit(solution)/shard_map/all_to_all | solution.py:306
  19.4 0.0 collective-permute-done
  19.4 0.1 collective-permute-start.1
  19.5 1.5 %collective-permute-done.1 = bf16[8,128,128]{2,1,0:T(8,128)(2,1)S(1)} collective-permute-done((bf16[8,128,128]{2,1,0:T(8,128)(2,1)S(1)}, bf16[8,128,128]{2,1,0:T(8,128)(2,1)S(1)}, u32[]{:S(2)}, u32[]{:S(2)}) %collective-permute-start.1) | collective-permute-done | bytes 262176 | tf_op jit(solution)/shard_map/ppermute | solution.py:293
  21.1 0.0 copy-done.3
  21.1 0.1 pad_maximum_fusion
  21.2 0.0 copy-done
  21.2 0.8 %fusion = bf16[1,8,128,128]{3,1,2,0:T(8,128)(2,1)S(1)} fusion(f32[8,24]{1,0:T(8,128)S(1)} %copy-done, bf16[3,8,128,128]{3,2,1,0:T(8,128)(2,1)S(1)} %bitcast.38), kind=kOutput, calls=%fused_computation.1 | convolution fusion | flops 37879808 | bytes 1049344 | tf_op jit(solution)/shard_map/dot_general | solution.py:310
  22.0 0.0 copy-start.4
  22.0 6.1 %all-to-all-done.parts_ref = bf16[16,128,128]{2,1,0:T(8,128)(2,1)S(1)} async-done(((bf16[16,128,128]{2,1,0:T(8,128)(2,1)}), bf16[16,128,128]{2,1,0:T(8,128)(2,1)S(1)}, u32[]{:S(2)}, u32[]{:S(2)}) %all-to-all-start) | async-done | bytes 524320 | tf_op jit(solution)/shard_map/all_to_all | solution.py:306
  28.1 0.1 near_sums.1.refs_1_
  28.2 0.9 %collective-permute-start.2 = (bf16[128,128]{1,0:T(8,128)(2,1)S(1)}, bf16[128,128]{1,0:T(8,128)(2,1)S(1)}, u32[]{:S(2)}, u32[]{:S(2)}) collective-permute-start(bf16[128,128]{1,0:T(8,128)(2,1)S(1)} %near_sums.1.refs_1_), channel_id=1, source_target_pairs={{0,16},{8,24},{16,0},{24,8},{1,17},{9,25},{17,1},{25,9},{2,18},{10... | collective-permute-start | bytes 98312 | tf_op jit(solution)/shard_map/ppermute | solution.py:317
  29.1 0.6 collective-permute-start.3
  29.6 4.3 %collective-permute-start.4 = (bf16[128,128]{1,0:T(8,128)(2,1)S(1)}, bf16[128,128]{1,0:T(8,128)(2,1)S(1)}, u32[]{:S(2)}, u32[]{:S(2)}) collective-permute-start(bf16[128,128]{1,0:T(8,128)(2,1)S(1)} %near_sums.1.refs_1_), channel_id=1, source_target_pairs={{0,8},{8,0},{16,24},{24,16},{1,9},{9,1},{17,25},{25,17},{2,10},{10... | collective-permute-start | bytes 98312 | tf_op jit(solution)/shard_map/ppermute | solution.py:317
  33.9 0.0 copy-start.1
  33.9 2.2 %copy-done.1 = bf16[16,8,128,128]{3,2,1,0:T(8,128)(2,1)S(1)} copy-done((bf16[16,8,128,128]{3,2,1,0:T(8,128)(2,1)S(1)}, bf16[16,8,128,128]{3,2,1,0:T(8,128)(2,1)}, u32[]{:S(2)}) %copy-start.1) | copy-done | bytes 4194328
  36.1 0.0 copy-start.2
  36.1 0.1 stacked_weights.1.refs_3_
  36.3 0.0 collective-permute-done.2.refs_2_
  36.3 0.0 collective-permute-done.3.refs_3_
  36.3 0.0 collective-permute-done.4.refs_4_
  36.3 0.2 normed_copies.1
  36.5 14.6 %all_to_all.10.refs_2_ = bf16[16,144,128]{2,1,0:T(8,128)(2,1)S(1)} all-to-all(bf16[16,144,128]{2,1,0:T(8,128)(2,1)S(1)} %normed_copies.1), channel_id=1, replica_groups=mesh['yh'=2,'x'=4,'zh'=4,'zl'=2,'yl'=2,'core'=2] {'yh','x','zl'}, dimensions={0} | all-to-all | bytes 1179648 | tf_op jit(solution)/shard_map/all_to_all | solution.py:327
  51.2 0.0 copy-done.4
  51.2 0.0 copy-done.2
  51.2 3.3 %residual.2.refs_4_ = bf16[16,8,128,128]{3,2,1,0:T(8,128)(2,1)} custom-call(s32[1]{0:T(128)} %bitcast.4.core_ref, s32[8,16]{1,0:T(8,128)S(1)} %bitcast.36, bf16[16,8,128,128]{3,2,1,0:T(8,128)(2,1)S(1)} %copy-done.2, bf16[16,144,128]{2,1,0:T(8,128)(2,1)S(1)} %all_to_all.10.refs_2_, bf16[6,256,256]{2,1,0:T(8,128)(2,1)S(1)} %stacked_weights.1.refs_3_), custom_call_target="tpu_custom_call" | custom-call | flops 1073741824 | bytes 8388608 | tf_op jit(solution)/shard_map/residual/pallas_call | solution.py:249
  54.6 0.5 collective-permute-start.5
  55.1 1.7 %collective-permute-start.6 = (f32[4,2,128]{2,1,0:T(2,128)S(1)}, f32[4,2,128]{2,1,0:T(2,128)S(1)}, u32[]{:S(2)}, u32[]{:S(2)}) collective-permute-start(f32[4,2,128]{2,1,0:T(2,128)S(1)} %get-tuple-element.40), channel_id=1, source_target_pairs={{0,3},{1,2},{2,1},{3,0},{4,7},{5,6},{6,5},{7,4},{8,11},{9,10},{10,... | collective-permute-start | bytes 12296 | tf_op jit(solution)/shard_map/ppermute | solution.py:282
  56.8 0.0 collective-permute-start.7
  56.8 0.2 residual.3
  56.9 0.2 collective-permute-done.5
  57.1 1.2 %collective-permute-done.6 = f32[4,2,128]{2,1,0:T(2,128)S(1)} collective-permute-done((f32[4,2,128]{2,1,0:T(2,128)S(1)}, f32[4,2,128]{2,1,0:T(2,128)S(1)}, u32[]{:S(2)}, u32[]{:S(2)}) %collective-permute-start.6) | collective-permute-done | bytes 4128 | tf_op jit(solution)/shard_map/ppermute | solution.py:282
  58.3 0.0 collective-permute-done.7
  58.3 0.6 fusion.6
  (6 shorter events, 0.1 us)
Async XLA Ops:
  0.6 20.5 %copy-start = (f32[8,24]{1,0:T(8,128)S(1)}, f32[8,24]{1,0:T(8,128)}, u32[]{:S(2)}) copy-start(f32[8,24]{1,0:T(8,128)} %param.7) | copy-start | bytes 2308
  0.6 20.4 %copy-start.3 = (bf16[8,128,128]{2,1,0:T(8,128)(2,1)S(1)}, bf16[8,128,128]{2,1,0:T(8,128)(2,1)}, u32[]{:S(2)}) copy-start(bf16[8,128,128]{2,1,0:T(8,128)(2,1)} %panels_ref.1) | copy-start | bytes 786436
  0.7 18.7 %collective-permute-start = (bf16[8,128,128]{2,1,0:T(8,128)(2,1)}, bf16[8,128,128]{2,1,0:T(8,128)(2,1)S(1)}, u32[]{:S(2)}, u32[]{:S(2)}) collective-permute-start(bf16[8,128,128]{2,1,0:T(8,128)(2,1)} %panels_ref.1), channel_id=1, source_target_pairs={{0,4},{4,8},{8,12},{12,16},{16,20},{20,24},{24,28},{28,32},{32,36}... | collective-permute-start | bytes 786440 | tf_op jit(solution)/shard_map/ppermute | solution.py:292
  15.8 12.3 %all-to-all-start = ((bf16[16,128,128]{2,1,0:T(8,128)(2,1)}), bf16[16,128,128]{2,1,0:T(8,128)(2,1)S(1)}, u32[]{:S(2)}, u32[]{:S(2)}) async-start(bf16[16,128,128]{2,1,0:T(8,128)(2,1)} %bitcast.39), calls=%async_computation | async-start | bytes 1048576 | tf_op jit(solution)/shard_map/all_to_all | solution.py:306
  19.4 1.6 %collective-permute-start.1 = (bf16[8,128,128]{2,1,0:T(8,128)(2,1)S(1)}, bf16[8,128,128]{2,1,0:T(8,128)(2,1)S(1)}, u32[]{:S(2)}, u32[]{:S(2)}) collective-permute-start(bf16[8,128,128]{2,1,0:T(8,128)(2,1)S(1)} %collective-permute-done), channel_id=1, source_target_pairs={{0,1},{1,0},{2,3},{3,2},{4,5},{5,4},{6,7},{7,6},{8,9},{9,8},{10,11... | collective-permute-start | bytes 786440 | tf_op jit(solution)/shard_map/ppermute | solution.py:293
  22.0 29.3 %copy-start.4 = (s32[16,8]{0,1:T(8,128)S(1)}, s32[16,8]{0,1:T(8,128)}, u32[]{:S(2)}) copy-start(s32[16,8]{0,1:T(8,128)} %param.5) | copy-start | bytes 1540
  28.2 8.1 %collective-permute-start.2 = (bf16[128,128]{1,0:T(8,128)(2,1)S(1)}, bf16[128,128]{1,0:T(8,128)(2,1)S(1)}, u32[]{:S(2)}, u32[]{:S(2)}) collective-permute-start(bf16[128,128]{1,0:T(8,128)(2,1)S(1)} %near_sums.1.refs_1_), channel_id=1, source_target_pairs={{0,16},{8,24},{16,0},{24,8},{1,17},{9,25},{17,1},{25,9},{2,18},{10... | collective-permute-start | bytes 98312 | tf_op jit(solution)/shard_map/ppermute | solution.py:317
  29.1 7.2 %collective-permute-start.3 = (bf16[128,128]{1,0:T(8,128)(2,1)S(1)}, bf16[128,128]{1,0:T(8,128)(2,1)S(1)}, u32[]{:S(2)}, u32[]{:S(2)}) collective-permute-start(bf16[128,128]{1,0:T(8,128)(2,1)S(1)} %near_sums.1.refs_1_), channel_id=1, source_target_pairs={{0,24},{8,16},{16,8},{24,0},{1,25},{9,17},{17,9},{25,1},{2,26},{10... | collective-permute-start | bytes 98312 | tf_op jit(solution)/shard_map/ppermute | solution.py:317
  29.6 6.7 %collective-permute-start.4 = (bf16[128,128]{1,0:T(8,128)(2,1)S(1)}, bf16[128,128]{1,0:T(8,128)(2,1)S(1)}, u32[]{:S(2)}, u32[]{:S(2)}) collective-permute-start(bf16[128,128]{1,0:T(8,128)(2,1)S(1)} %near_sums.1.refs_1_), channel_id=1, source_target_pairs={{0,8},{8,0},{16,24},{24,16},{1,9},{9,1},{17,25},{25,17},{2,10},{10... | collective-permute-start | bytes 98312 | tf_op jit(solution)/shard_map/ppermute | solution.py:317
  33.9 2.2 %copy-start.1 = (bf16[16,8,128,128]{3,2,1,0:T(8,128)(2,1)S(1)}, bf16[16,8,128,128]{3,2,1,0:T(8,128)(2,1)}, u32[]{:S(2)}) copy-start(bf16[16,8,128,128]{3,2,1,0:T(8,128)(2,1)} %refs_1_.5) | copy-start | bytes 12582916
  36.1 15.1 %copy-start.2 = (bf16[16,8,128,128]{3,2,1,0:T(8,128)(2,1)S(1)}, bf16[16,8,128,128]{3,2,1,0:T(8,128)(2,1)}, u32[]{:S(2)}) copy-start(bf16[16,8,128,128]{3,2,1,0:T(8,128)(2,1)} %refs_1_.5) | copy-start | bytes 12582916
  54.6 2.5 %collective-permute-start.5 = (f32[4,2,128]{2,1,0:T(2,128)S(1)}, f32[4,2,128]{2,1,0:T(2,128)S(1)}, u32[]{:S(2)}, u32[]{:S(2)}) collective-permute-start(f32[4,2,128]{2,1,0:T(2,128)S(1)} %get-tuple-element.38), channel_id=1, source_target_pairs={{0,2},{1,3},{2,0},{3,1},{4,6},{5,7},{6,4},{7,5},{8,10},{9,11},{10,... | collective-permute-start | bytes 12296 | tf_op jit(solution)/shard_map/ppermute | solution.py:282
  55.1 3.3 %collective-permute-start.6 = (f32[4,2,128]{2,1,0:T(2,128)S(1)}, f32[4,2,128]{2,1,0:T(2,128)S(1)}, u32[]{:S(2)}, u32[]{:S(2)}) collective-permute-start(f32[4,2,128]{2,1,0:T(2,128)S(1)} %get-tuple-element.40), channel_id=1, source_target_pairs={{0,3},{1,2},{2,1},{3,0},{4,7},{5,6},{6,5},{7,4},{8,11},{9,10},{10,... | collective-permute-start | bytes 12296 | tf_op jit(solution)/shard_map/ppermute | solution.py:282
  56.8 1.6 %collective-permute-start.7 = (f32[4,2,128]{2,1,0:T(2,128)S(1)}, f32[4,2,128]{2,1,0:T(2,128)S(1)}, u32[]{:S(2)}, u32[]{:S(2)}) collective-permute-start(f32[4,2,128]{2,1,0:T(2,128)S(1)} %get-tuple-element.39), channel_id=1, source_target_pairs={{0,1},{1,0},{2,3},{3,2},{4,5},{5,4},{6,7},{7,6},{8,9},{9,8},{10,11... | collective-permute-start | bytes 12296 | tf_op jit(solution)/shard_map/ppermute | solution.py:282

commit v8 on v7

--- a/solution.py
+++ b/solution.py
@@ -302,7 +302,8 @@
     rows = width // vir_count
     flags = active.T
     partial = partial_sums(flags, l3_tiles, panels)
-    before, after = halo(panels)
+    partial, sent = lax.optimization_barrier((partial, panels))
+    before, after = halo(sent)
     parts = lax.all_to_all(partial.reshape(near, -1, width), NEAR, 0, 0, tiled=True)
 
     window = jnp.concatenate([before, panels, after], axis=0)

time: 59.8 us -> 59.5 us (level)
  starting transfers between devices: 22.9 us -> 24.5 us
  waiting for transfers between devices: 9.05 us -> 7.45 us
    ppermute x1, starting transfers between devices: 0.09 us -> 1.71 us  [halo(): other = lax.ppermute(mine, 'core', [(0, 1), (1, 0)])]
    all_to_all x1, waiting for transfers between devices: 6.1 us -> 4.85 us  [shards(): lax.all_to_all(partial.reshape(near, -1, width), NEAR, 0, 0, tiled=True)]
  transfers between devices with their start and end apart: 9 -> 9, of which waited for: 4 -> 4; matrix products, arithmetic and copies ran while one was open for 2% -> 2% of each run, Pallas kernels for 7% -> 0%
where the time goes in v8:
time: 59.5 us; the launch traced here: 59 us
  starting transfers between devices  24.5 us (41%)
  blocking collectives  14.6 us (25%)
  Pallas kernels  7.77 us (13%)
  waiting for transfers between devices  7.45 us (13%)
  local copies, waits for them, and re-layouts  2.27 us (4%)
  between operations  0.82 us (1%)
  matrix products  0.76 us (1%)
  other arithmetic  0.74 us (1%)
    all_to_all x1, blocking collectives, shards(): gathered = lax.all_to_all(copies, NEAR, 0, 0, tiled=True)  14.6 us
    ppermute x1, starting transfers between devices, halo(): mine = lax.ppermute(panels, (*VIR, 'core'), pairs)  11.3 us
    ppermute x3, starting transfers between devices, shards(): parts.append(lax.ppermute(part, 'zh', [(i, i ^ step) for i in range(far)]))  5.74 us
    all_to_all x1, waiting for transfers between devices, shards(): lax.all_to_all(partial.reshape(near, -1, width), NEAR, 0, 0, tiled=True)  4.85 us
    pallas_call x1, Pallas kernels, partial_sums(): pl.pallas_call(kernel, in_specs=[pl.BlockSpec(memory_space=pltpu.HBM)] *...  3.87 us
    all_to_all x1, starting transfers between devices, shards(): lax.all_to_all(partial.reshape(near, -1, width), NEAR, 0, 0, tiled=True)  3.57 us
    pallas_call x2, Pallas kernels, residual(): pl.pallas_call(kernel, in_specs=in_specs, out_specs=hbm, out_shape=jax.Sh...  3.47 us
    unnamed x11, local copies, waits for them, and re-layouts  2.25 us
  transfers between devices with their start and end apart: 9, of which 4 were waited for; matrix products, arithmetic and copies ran while one was open for 2% of the time, Pallas kernels for 0%

profile of v8, /device:TPU:1, one launch (start us, length us, event | category | flops | bytes accessed | tf_op | source)
XLA Modules:
  0.0 59.0 jit_solution(18162196340207277806)
XLA Ops:
  0.6 0.0 copy-start
  0.6 0.0 copy-start.3
  0.7 3.9 %partial_sums.1 = bf16[2048,128]{1,0:T(8,128)(2,1)} custom-call(s32[8,16]{1,0:T(8,128)} %bitcast.35, bf16[16,8,128,128]{3,2,1,0:T(8,128)(2,1)} %refs_1_.5, bf16[8,128,128]{2,1,0:T(8,128)(2,1)} %panels_ref.1), custom_call_target="tpu_custom_call" | custom-call | flops 536870912 | bytes 4194304 | tf_op jit(solution)/shard_map/partial_sums/pallas_call | solution.py:77
  4.5 0.0 copy-done.3
  4.5 11.3 %collective-permute-start = (bf16[8,128,128]{2,1,0:T(8,128)(2,1)S(1)}, bf16[8,128,128]{2,1,0:T(8,128)(2,1)S(1)}, u32[]{:S(2)}, u32[]{:S(2)}) collective-permute-start(bf16[8,128,128]{2,1,0:T(8,128)(2,1)S(1)} %copy-done.3), channel_id=1, source_target_pairs={{0,4},{4,8},{8,12},{12,16},{16,20},{20,24},{24,28},{28,32},{32,36}... | collective-permute-start | bytes 786440 | tf_op jit(solution)/shard_map/ppermute | solution.py:292
  15.9 3.6 %all-to-all-start = ((bf16[16,128,128]{2,1,0:T(8,128)(2,1)}), bf16[16,128,128]{2,1,0:T(8,128)(2,1)S(1)}, u32[]{:S(2)}, u32[]{:S(2)}) async-start(bf16[16,128,128]{2,1,0:T(8,128)(2,1)} %bitcast.39), calls=%async_computation | async-start | bytes 1048576 | tf_op jit(solution)/shard_map/all_to_all | solution.py:307
  19.4 0.0 collective-permute-done
  19.4 1.7 %collective-permute-start.1 = (bf16[8,128,128]{2,1,0:T(8,128)(2,1)S(1)}, bf16[8,128,128]{2,1,0:T(8,128)(2,1)S(1)}, u32[]{:S(2)}, u32[]{:S(2)}) collective-permute-start(bf16[8,128,128]{2,1,0:T(8,128)(2,1)S(1)} %collective-permute-done), channel_id=1, source_target_pairs={{0,1},{1,0},{2,3},{3,2},{4,5},{5,4},{6,7},{7,6},{8,9},{9,8},{10,11... | collective-permute-start | bytes 786440 | tf_op jit(solution)/shard_map/ppermute | solution.py:293
  21.2 1.2 %collective-permute-done.1 = bf16[8,128,128]{2,1,0:T(8,128)(2,1)S(1)} collective-permute-done((bf16[8,128,128]{2,1,0:T(8,128)(2,1)S(1)}, bf16[8,128,128]{2,1,0:T(8,128)(2,1)S(1)}, u32[]{:S(2)}, u32[]{:S(2)}) %collective-permute-start.1) | collective-permute-done | bytes 262176 | tf_op jit(solution)/shard_map/ppermute | solution.py:293
  22.4 0.1 pad_maximum_fusion
  22.5 0.0 copy-done
  22.5 0.8 %fusion = bf16[1,8,128,128]{3,1,2,0:T(8,128)(2,1)S(1)} fusion(f32[8,24]{1,0:T(8,128)S(1)} %copy-done, bf16[3,8,128,128]{3,2,1,0:T(8,128)(2,1)S(1)} %bitcast.38), kind=kOutput, calls=%fused_computation.1 | convolution fusion | flops 37879808 | bytes 1049344 | tf_op jit(solution)/shard_map/dot_general | solution.py:311
  23.2 0.0 copy-start.4
  23.3 4.9 %all-to-all-done.parts_ref = bf16[16,128,128]{2,1,0:T(8,128)(2,1)S(1)} async-done(((bf16[16,128,128]{2,1,0:T(8,128)(2,1)}), bf16[16,128,128]{2,1,0:T(8,128)(2,1)S(1)}, u32[]{:S(2)}, u32[]{:S(2)}) %all-to-all-start) | async-done | bytes 524320 | tf_op jit(solution)/shard_map/all_to_all | solution.py:307
  28.2 0.1 near_sums.1.refs_1_
  28.2 0.9 %collective-permute-start.2 = (bf16[128,128]{1,0:T(8,128)(2,1)S(1)}, bf16[128,128]{1,0:T(8,128)(2,1)S(1)}, u32[]{:S(2)}, u32[]{:S(2)}) collective-permute-start(bf16[128,128]{1,0:T(8,128)(2,1)S(1)} %near_sums.1.refs_1_), channel_id=1, source_target_pairs={{0,16},{8,24},{16,0},{24,8},{1,17},{9,25},{17,1},{25,9},{2,18},{10... | collective-permute-start | bytes 98312 | tf_op jit(solution)/shard_map/ppermute | solution.py:318
  29.1 0.6 collective-permute-start.3
  29.7 4.3 %collective-permute-start.4 = (bf16[128,128]{1,0:T(8,128)(2,1)S(1)}, bf16[128,128]{1,0:T(8,128)(2,1)S(1)}, u32[]{:S(2)}, u32[]{:S(2)}) collective-permute-start(bf16[128,128]{1,0:T(8,128)(2,1)S(1)} %near_sums.1.refs_1_), channel_id=1, source_target_pairs={{0,8},{8,0},{16,24},{24,16},{1,9},{9,1},{17,25},{25,17},{2,10},{10... | collective-permute-start | bytes 98312 | tf_op jit(solution)/shard_map/ppermute | solution.py:318
  34.0 0.0 copy-start.1
  34.0 2.2 %copy-done.1 = bf16[16,8,128,128]{3,2,1,0:T(8,128)(2,1)S(1)} copy-done((bf16[16,8,128,128]{3,2,1,0:T(8,128)(2,1)S(1)}, bf16[16,8,128,128]{3,2,1,0:T(8,128)(2,1)}, u32[]{:S(2)}) %copy-start.1) | copy-done | bytes 4194328
  36.2 0.0 copy-start.2
  36.2 0.1 stacked_weights.1.refs_3_
  36.3 0.0 collective-permute-done.2.refs_2_
  36.3 0.0 collective-permute-done.3.refs_3_
  36.3 0.0 collective-permute-done.4.refs_4_
  36.3 0.2 normed_copies.1
  36.6 14.6 %all_to_all.10.refs_2_ = bf16[16,144,128]{2,1,0:T(8,128)(2,1)S(1)} all-to-all(bf16[16,144,128]{2,1,0:T(8,128)(2,1)S(1)} %normed_copies.1), channel_id=1, replica_groups=mesh['yh'=2,'x'=4,'zh'=4,'zl'=2,'yl'=2,'core'=2] {'yh','x','zl'}, dimensions={0} | all-to-all | bytes 1179648 | tf_op jit(solution)/shard_map/all_to_all | solution.py:328
  51.2 0.0 copy-done.4
  51.3 0.0 copy-done.2
  51.3 3.3 %residual.2.refs_4_ = bf16[16,8,128,128]{3,2,1,0:T(8,128)(2,1)} custom-call(s32[1]{0:T(128)} %bitcast.4.core_ref, s32[8,16]{1,0:T(8,128)S(1)} %bitcast.36, bf16[16,8,128,128]{3,2,1,0:T(8,128)(2,1)S(1)} %copy-done.2, bf16[16,144,128]{2,1,0:T(8,128)(2,1)S(1)} %all_to_all.10.refs_2_, bf16[6,256,256]{2,1,0:T(8,128)(2,1)S(1)} %stacked_weights.1.refs_3_), custom_call_target="tpu_custom_call" | custom-call | flops 1073741824 | bytes 8388608 | tf_op jit(solution)/shard_map/residual/pallas_call | solution.py:249
  54.6 0.5 collective-permute-start.5
  55.1 1.7 %collective-permute-start.6 = (f32[4,2,128]{2,1,0:T(2,128)S(1)}, f32[4,2,128]{2,1,0:T(2,128)S(1)}, u32[]{:S(2)}, u32[]{:S(2)}) collective-permute-start(f32[4,2,128]{2,1,0:T(2,128)S(1)} %get-tuple-element.44), channel_id=1, source_target_pairs={{0,3},{1,2},{2,1},{3,0},{4,7},{5,6},{6,5},{7,4},{8,11},{9,10},{10,... | collective-permute-start | bytes 12296 | tf_op jit(solution)/shard_map/ppermute | solution.py:282
  56.8 0.0 collective-permute-start.7
  56.8 0.2 residual.3
  57.0 0.2 collective-permute-done.5
  57.2 1.2 %collective-permute-done.6 = f32[4,2,128]{2,1,0:T(2,128)S(1)} collective-permute-done((f32[4,2,128]{2,1,0:T(2,128)S(1)}, f32[4,2,128]{2,1,0:T(2,128)S(1)}, u32[]{:S(2)}, u32[]{:S(2)}) %collective-permute-start.6) | collective-permute-done | bytes 4128 | tf_op jit(solution)/shard_map/ppermute | solution.py:282
  58.4 0.0 collective-permute-done.7
  58.4 0.6 fusion.6
  (6 shorter events, 0.1 us)
Async XLA Ops:
  0.6 21.8 %copy-start = (f32[8,24]{1,0:T(8,128)S(1)}, f32[8,24]{1,0:T(8,128)}, u32[]{:S(2)}) copy-start(f32[8,24]{1,0:T(8,128)} %param.7) | copy-start | bytes 2308
  0.6 3.9 %copy-start.3 = (bf16[8,128,128]{2,1,0:T(8,128)(2,1)S(1)}, bf16[8,128,128]{2,1,0:T(8,128)(2,1)}, u32[]{:S(2)}) copy-start(bf16[8,128,128]{2,1,0:T(8,128)(2,1)} %panels_ref.1) | copy-start | bytes 786436
  4.5 14.9 %collective-permute-start = (bf16[8,128,128]{2,1,0:T(8,128)(2,1)S(1)}, bf16[8,128,128]{2,1,0:T(8,128)(2,1)S(1)}, u32[]{:S(2)}, u32[]{:S(2)}) collective-permute-start(bf16[8,128,128]{2,1,0:T(8,128)(2,1)S(1)} %copy-done.3), channel_id=1, source_target_pairs={{0,4},{4,8},{8,12},{12,16},{16,20},{20,24},{24,28},{28,32},{32,36}... | collective-permute-start | bytes 786440 | tf_op jit(solution)/shard_map/ppermute | solution.py:292
  15.9 12.3 %all-to-all-start = ((bf16[16,128,128]{2,1,0:T(8,128)(2,1)}), bf16[16,128,128]{2,1,0:T(8,128)(2,1)S(1)}, u32[]{:S(2)}, u32[]{:S(2)}) async-start(bf16[16,128,128]{2,1,0:T(8,128)(2,1)} %bitcast.39), calls=%async_computation | async-start | bytes 1048576 | tf_op jit(solution)/shard_map/all_to_all | solution.py:307
  19.4 2.9 %collective-permute-start.1 = (bf16[8,128,128]{2,1,0:T(8,128)(2,1)S(1)}, bf16[8,128,128]{2,1,0:T(8,128)(2,1)S(1)}, u32[]{:S(2)}, u32[]{:S(2)}) collective-permute-start(bf16[8,128,128]{2,1,0:T(8,128)(2,1)S(1)} %collective-permute-done), channel_id=1, source_target_pairs={{0,1},{1,0},{2,3},{3,2},{4,5},{5,4},{6,7},{7,6},{8,9},{9,8},{10,11... | collective-permute-start | bytes 786440 | tf_op jit(solution)/shard_map/ppermute | solution.py:293
  23.2 28.0 %copy-start.4 = (s32[16,8]{0,1:T(8,128)S(1)}, s32[16,8]{0,1:T(8,128)}, u32[]{:S(2)}) copy-start(s32[16,8]{0,1:T(8,128)} %param.5) | copy-start | bytes 1540
  28.2 8.1 %collective-permute-start.2 = (bf16[128,128]{1,0:T(8,128)(2,1)S(1)}, bf16[128,128]{1,0:T(8,128)(2,1)S(1)}, u32[]{:S(2)}, u32[]{:S(2)}) collective-permute-start(bf16[128,128]{1,0:T(8,128)(2,1)S(1)} %near_sums.1.refs_1_), channel_id=1, source_target_pairs={{0,16},{8,24},{16,0},{24,8},{1,17},{9,25},{17,1},{25,9},{2,18},{10... | collective-permute-start | bytes 98312 | tf_op jit(solution)/shard_map/ppermute | solution.py:318
  29.1 7.2 %collective-permute-start.3 = (bf16[128,128]{1,0:T(8,128)(2,1)S(1)}, bf16[128,128]{1,0:T(8,128)(2,1)S(1)}, u32[]{:S(2)}, u32[]{:S(2)}) collective-permute-start(bf16[128,128]{1,0:T(8,128)(2,1)S(1)} %near_sums.1.refs_1_), channel_id=1, source_target_pairs={{0,24},{8,16},{16,8},{24,0},{1,25},{9,17},{17,9},{25,1},{2,26},{10... | collective-permute-start | bytes 98312 | tf_op jit(solution)/shard_map/ppermute | solution.py:318
  29.7 6.7 %collective-permute-start.4 = (bf16[128,128]{1,0:T(8,128)(2,1)S(1)}, bf16[128,128]{1,0:T(8,128)(2,1)S(1)}, u32[]{:S(2)}, u32[]{:S(2)}) collective-permute-start(bf16[128,128]{1,0:T(8,128)(2,1)S(1)} %near_sums.1.refs_1_), channel_id=1, source_target_pairs={{0,8},{8,0},{16,24},{24,16},{1,9},{9,1},{17,25},{25,17},{2,10},{10... | collective-permute-start | bytes 98312 | tf_op jit(solution)/shard_map/ppermute | solution.py:318
  34.0 2.2 %copy-start.1 = (bf16[16,8,128,128]{3,2,1,0:T(8,128)(2,1)S(1)}, bf16[16,8,128,128]{3,2,1,0:T(8,128)(2,1)}, u32[]{:S(2)}) copy-start(bf16[16,8,128,128]{3,2,1,0:T(8,128)(2,1)} %refs_1_.5) | copy-start | bytes 12582916
  36.2 15.1 %copy-start.2 = (bf16[16,8,128,128]{3,2,1,0:T(8,128)(2,1)S(1)}, bf16[16,8,128,128]{3,2,1,0:T(8,128)(2,1)}, u32[]{:S(2)}) copy-start(bf16[16,8,128,128]{3,2,1,0:T(8,128)(2,1)} %refs_1_.5) | copy-start | bytes 12582916
  54.6 2.5 %collective-permute-start.5 = (f32[4,2,128]{2,1,0:T(2,128)S(1)}, f32[4,2,128]{2,1,0:T(2,128)S(1)}, u32[]{:S(2)}, u32[]{:S(2)}) collective-permute-start(f32[4,2,128]{2,1,0:T(2,128)S(1)} %get-tuple-element.42), channel_id=1, source_target_pairs={{0,2},{1,3},{2,0},{3,1},{4,6},{5,7},{6,4},{7,5},{8,10},{9,11},{10,... | collective-permute-start | bytes 12296 | tf_op jit(solution)/shard_map/ppermute | solution.py:282
  55.1 3.3 %collective-permute-start.6 = (f32[4,2,128]{2,1,0:T(2,128)S(1)}, f32[4,2,128]{2,1,0:T(2,128)S(1)}, u32[]{:S(2)}, u32[]{:S(2)}) collective-permute-start(f32[4,2,128]{2,1,0:T(2,128)S(1)} %get-tuple-element.44), channel_id=1, source_target_pairs={{0,3},{1,2},{2,1},{3,0},{4,7},{5,6},{6,5},{7,4},{8,11},{9,10},{10,... | collective-permute-start | bytes 12296 | tf_op jit(solution)/shard_map/ppermute | solution.py:282
  56.8 1.6 %collective-permute-start.7 = (f32[4,2,128]{2,1,0:T(2,128)S(1)}, f32[4,2,128]{2,1,0:T(2,128)S(1)}, u32[]{:S(2)}, u32[]{:S(2)}) collective-permute-start(f32[4,2,128]{2,1,0:T(2,128)S(1)} %get-tuple-element.43), channel_id=1, source_target_pairs={{0,1},{1,0},{2,3},{3,2},{4,5},{5,4},{6,7},{7,6},{8,9},{9,8},{10,11... | collective-permute-start | bytes 12296 | tf_op jit(solution)/shard_map/ppermute | solution.py:282
